TPU v7x, 32 devices: a whole 2x2x4 slice. The times are simulated.
32 devices in a mesh: wide: 8 (over z, x), narrow: 4 (over y, core).
Axes of the slice: x: 2, y: 2, z: 4, core: 2. Of those that a mesh axis runs over, the one named last changes fastest.
Arguments:
- tokens: bfloat16 [2, 32768, 512], P(None, ('wide', 'narrow')), may hold values from -6 to 6
- out_grad: bfloat16 [2, 32768, 512], P(None, ('wide', 'narrow')), may hold values from -6 to 6
- long_count: int32 [2, 32], P(None, ('wide', 'narrow')), may hold values from 0 to 1
- params: float32 [3676160], P(('wide', 'narrow')), may hold values from -3 to 3, as said below
Outputs:
- outputs: bfloat16 [2, 32768, 512], P(None, ('wide', 'narrow'))
- input_grad: bfloat16 [2, 32768, 512], P(None, ('wide', 'narrow'))
- param_grad: float32 [3676160], P(('wide', 'narrow'))
Inputs may be any that keep to these rules, and one draw needn't show every extreme that they name: `params`: the packed parameters, laid out as the first step states.
All inputs are finite; a program needn't handle non-finite values.
Results may differ from a plain program's by a relative error of at most 0.011.
Values may be sent and summed in bfloat16 or wider, within the bound.
No kernel may reach another device: no remote copies, remote signals or barrier semaphores. Data moves between devices by JAX's collectives and lax.ppermute only.
A program may use at most 192 MiB of HBM per device.

v0:
```python
import functools
import math

import jax
import jax.numpy as jnp
from jax import lax
from jax.experimental import pallas as pl
from jax.experimental.pallas import tpu as pltpu
from jax.sharding import Mesh, PartitionSpec as P

D = 512
FF = 2048
HEADS = 8
HD = 64
SHORT = 512
LONG = 1024
PAIR = 2 * HD
GROUP = 2 * PAIR
GROUPS = D // GROUP
STRIP = 256

TILE_ROWS = 16
TILE = TILE_ROWS * D

layer_eps = 1e-05
far_below = -1e30

F32 = jnp.float32
BF16 = jnp.bfloat16
MB = 1024 * 1024


def dot_nn(left, right):
    return lax.dot_general(left, right, (((1,), (0,)), ((), ())), preferred_element_type=F32)


def dot_nt(left, right):
    return lax.dot_general(left, right, (((1,), (1,)), ((), ())), preferred_element_type=F32)


def dot_tn(left, right):
    return lax.dot_general(left, right, (((0,), (0,)), ((), ())), preferred_element_type=F32)


def layer_stats(values):
    average = jnp.mean(values, -1, keepdims=True)
    centred = values - average
    variance = jnp.mean(centred * centred, -1, keepdims=True)
    inv_std = lax.rsqrt(variance + layer_eps)
    return (centred * inv_std, inv_std)


def norm_back(grad_hat, normed, inv_std):
    return inv_std * (
        grad_hat
        - jnp.mean(grad_hat, -1, keepdims=True)
        - normed * jnp.mean(grad_hat * normed, -1, keepdims=True)
    )


def sigmoid(values):
    return 0.5 * jnp.tanh(0.5 * values) + 0.5


def fold_rows(values):
    return jnp.sum(values.reshape(values.shape[0] // 8, 8, values.shape[1]), 0)


ROW_QUERY = 0
ROW_KEY = 512
ROW_VALUE = 1024
ROW_OUT = 1536
ROW_GATE_A = 2048
ROW_GATE_F = 2560
ROW_IN = 3072
ROW_DOWN = 5120
ROW_VEC = 7168
ALL_ROWS = 7184
VEC_ROWS = 16
ENTRIES = 6 * D * D + 2 * D * FF + 8 * D + FF

SHARES = 32
PLANES = 4
IN_PLANE = SHARES // PLANES
HALF = IN_PLANE // 2
STARTS = [index * (ENTRIES // SHARES) // TILE * TILE_ROWS for index in range(SHARES)]
BLOCK = max(
    -(-((index + 1) * (ENTRIES // SHARES)) // TILE) * TILE_ROWS - STARTS[index] for index in range(SHARES)
)
PLANE_END = [STARTS[(plane + 1) * IN_PLANE - 1] + BLOCK for plane in range(PLANES)]
VEC_AT = ROW_VEC - STARTS[-1]

VMEM = pltpu.CompilerParams(vmem_limit_bytes=60 * MB)


def whole(shape, single=True):
    rank = len(shape)
    kwargs = {"pipeline_mode": pl.Buffered(1)} if single else {}
    return pl.BlockSpec(shape, lambda *unused: (0,) * rank, **kwargs)


def share_row(where, plane, spot, other):
    core = 1 - where[3] if other else where[3]
    share = 2 * ((where[1] * 2 + where[2]) ^ spot) + core
    return ((plane * IN_PLANE + share) * (ENTRIES // SHARES)) // TILE * TILE_ROWS


class Piece:
    def __init__(self, array, blocks, other, column):
        self.array, self.blocks, self.other, self.column = array, blocks, other, column


def place_piece(target, base, where, piece, source, lowest):
    width = min(source.shape[-1], target.shape[-1] - piece.column)

    def place(index, plane, spot):
        at = share_row(where, plane, spot, piece.other) - base
        rows = pl.ds(pl.multiple_of(at, TILE_ROWS), BLOCK)
        cols = slice(piece.column, piece.column + width)
        target[rows, cols] = target[rows, cols] + source[index, :BLOCK, :width]

    for index, (plane, spot) in enumerate(piece.blocks):
        if not isinstance(plane, tuple):
            if (plane == 0) == lowest:
                place(index, plane, spot)
            continue
        plane = where[plane[0]]
        pl.when((plane == 0) == lowest)(functools.partial(place, index, plane, spot))


UNREAD = pl.BlockSpec(memory_space=pl.ANY)


def call_kernel(body, arguments, through, in_specs, out_specs, out_shape, grid, name, cost, scalars=1, scratch=(), alias=None):
    inputs, outputs, passed = len(arguments), len(out_specs), len(through)
    aliases = {inputs + index: outputs + index for index in range(passed)}
    aliases.update(alias or {})

    def run(*refs):
        at = inputs + passed
        body(*refs[:inputs], *refs[at : at + outputs], *refs[at + outputs + passed :])

    results = pl.pallas_call(
        run,
        name=name,
        grid_spec=pltpu.PrefetchScalarGridSpec(
            num_scalar_prefetch=scalars,
            grid=grid,
            in_specs=list(in_specs) + [UNREAD] * passed,
            out_specs=list(out_specs) + [UNREAD] * passed,
            scratch_shapes=list(scratch),
        ),
        out_shape=list(out_shape) + [jax.ShapeDtypeStruct(array.shape, array.dtype) for array in through],
        input_output_aliases=aliases,
        compiler_params=VMEM,
        cost_estimate=pl.CostEstimate(flops=int(cost[0]), bytes_accessed=int(cost[1]), transcendentals=int(cost[2])),
    )(*arguments, *through)
    return results[:outputs], results[outputs:]


def emit_blocks(source, base, plane, where, keep, send):
    @pl.loop(0, HALF)
    def _(spot):
        for out, other in ((keep, False), (send, True)):
            at = share_row(where, plane, spot, other) - base
            out[spot] = source[pl.ds(pl.multiple_of(at, TILE_ROWS), BLOCK), :]


def split_three(values):
    high = values.astype(BF16)
    rest = values - high.astype(F32)
    middle = rest.astype(BF16)
    low = (rest - middle.astype(F32)).astype(BF16)
    return high, middle, low


def pick_lanes(base, lane, first, columns):
    out = base
    for offset, column in enumerate(columns):
        out = jnp.where(lane == first + offset, column, out)
    return out


def pipeline(units, *stages):
    held, results = {}, {}
    count = len(units)
    for turn in range(count + len(stages) - 1):
        for at in range(len(stages)):
            stage = (0, *range(len(stages) - 1, 0, -1))[at]
            unit = turn - stage
            if 0 <= unit < count:
                value = stages[stage](units[unit], *(held.pop(unit) if stage else ()))
                if stage + 1 < len(stages):
                    held[unit] = value
                else:
                    results[units[unit]] = value
    return results


def attend_columns(is_long, query, key, value, attended, extra):
    strips = LONG // STRIP
    key_ids = lax.broadcasted_iota(jnp.int32, (STRIP, STRIP), 0)
    query_ids = lax.broadcasted_iota(jnp.int32, (STRIP, STRIP), 1)
    causal = query_ids >= key_ids
    cut = jnp.where(is_long, 0.0, far_below)
    late = jnp.where(is_long, 0.0, 1.0)
    lane = lax.broadcasted_iota(jnp.int32, (LONG, PAIR), 1)
    ones = jnp.ones((TILE_ROWS, LONG), BF16)
    q_heads, k_pairs, v_heads = [], [], []
    for pair in range(query.shape[1] // PAIR):
        cols = slice(pair * PAIR, (pair + 1) * PAIR)
        rows = query[:, cols]
        zero = jnp.zeros_like(rows)
        q_heads += [jnp.where(lane < HD, rows, zero), jnp.where(lane >= HD, rows, zero)]
        k_pairs.append(key[:, cols])
        turned = value[:, cols].astype(F32).T.astype(BF16)
        v_heads += [jnp.concatenate([turned[:HD], ones], 0), jnp.concatenate([turned[HD:], ones], 0)]

    def scores_of(unit):
        strip, head = unit
        lo, reach = strip * STRIP, (strip + 1) * STRIP
        return (dot_nt(k_pairs[head // 2][:reach], q_heads[head][lo:reach]),)

    def soften(unit, scores):
        strip, unused = unit
        lo = strip * STRIP
        parts = []
        if lo >= SHORT:
            parts.append(scores[:SHORT] + cut)
            if lo > SHORT:
                parts.append(scores[SHORT:lo])
        elif strip:
            parts.append(scores[:lo])
        parts.append(jnp.where(causal, scores[lo:], far_below))
        scores = jnp.concatenate(parts, 0)
        largest = jnp.max(scores, 0, keepdims=True)
        return jnp.exp(scores - largest).astype(BF16), largest

    def finish(unit, shifted, largest):
        strip, head = unit
        out = dot_nn(v_heads[head][:, : (strip + 1) * STRIP], shifted)
        sum_exp = out[HD : HD + 1]
        return out[:HD] * (1.0 / sum_exp), largest + jnp.log(sum_exp)

    units = [(strip, head) for strip in range(strips) for head in range(len(q_heads))]
    results = pipeline(units, scores_of, soften, finish)
    for strip in range(strips):
        rows = slice(strip * STRIP, (strip + 1) * STRIP)
        for pair in range(len(k_pairs)):
            cols = slice(pair * PAIR, (pair + 1) * PAIR)
            two = [results[(strip, 2 * pair + side)] for side in range(2)]
            attended[rows, cols] = jnp.concatenate([out for out, unused in two], 0).T.astype(BF16)
            lines = [part.astype(F32) for unused, logsum in two for part in split_three(-logsum)]
            lines.append(jnp.broadcast_to(late if strip * STRIP >= SHORT else 0.0, (1, STRIP)))
            lines.append(jnp.zeros((PAIR - 7, STRIP), F32))
            extra[rows, cols] = jnp.concatenate(lines, 0).T.astype(BF16)


def forward_body(first, pieces, longs, where, rows_in, *rest):
    sources, rest = rest[: len(pieces)], rest[len(pieces) :]
    if first:
        query, key, value, attended, extra, w_three, w_out, hidden, vec, weights = rest
    else:
        query, key, value, attended, extra, w_three, w_out, weights = rest
    sub = pl.program_id(0)

    @pl.when(sub == 0)
    def _():
        weights[...] = jnp.zeros_like(weights)
        for piece, source in zip(pieces, sources):
            place_piece(weights, 0, where, piece, source, True)
        w_three[...] = weights[:ROW_OUT, :]
        w_out[...] = weights[ROW_OUT:, :]
        if first:
            total = jnp.zeros((VEC_ROWS, D), BF16)
            for source in sources:
                if source.shape[1] > BLOCK:
                    for index in range(source.shape[0]):
                        total = total + source[index, BLOCK:, :]
            vec[...] = total

    if first:
        normed, unused = layer_stats(rows_in[...].astype(F32))
        lines = vec[...].astype(F32)
        hid = (normed * lines[0:1] + lines[1:2]).astype(BF16)
        hidden[...] = hid
    else:
        hid = rows_in[...]
    q_rows = (dot_nn(hid, weights[ROW_QUERY : ROW_QUERY + D, :]) * (1.0 / math.sqrt(HD))).astype(BF16)
    k_rows = dot_nn(hid, weights[ROW_KEY : ROW_KEY + D, :]).astype(BF16)
    v_rows = dot_nn(hid, weights[ROW_VALUE : ROW_VALUE + D, :]).astype(BF16)
    query[...] = q_rows
    key[...] = k_rows
    value[...] = v_rows
    attend_columns(longs[sub] > 0, q_rows, k_rows, v_rows, attended, extra)


def forward_group(group, longs, where, rows_in, pieces, through):
    first = group == 0
    total = rows_in.shape[0]
    rows = pl.BlockSpec((LONG, D), lambda s, *refs: (s, 0))
    part = pl.BlockSpec((LONG, GROUP), lambda s, *refs: (s, 0))
    width = D if first else GROUP
    blocks = [
        pl.BlockSpec(piece.array.shape[:2] + (width,), lambda s, *refs: (0, 0, group), pipeline_mode=pl.Buffered(1))
        for piece in pieces
    ]
    tail = PLANE_END[0] - ROW_OUT
    out_specs = [part] * 5 + [whole((ROW_OUT, GROUP)), whole((tail, GROUP))]
    out_shape = [jax.ShapeDtypeStruct((total, GROUP), BF16)] * 5 + [
        jax.ShapeDtypeStruct((ROW_OUT, GROUP), BF16),
        jax.ShapeDtypeStruct((tail, GROUP), BF16),
    ]
    if first:
        out_specs += [rows, whole((VEC_ROWS, D))]
        out_shape += [jax.ShapeDtypeStruct((total, D), BF16), jax.ShapeDtypeStruct((VEC_ROWS, D), BF16)]
    return call_kernel(
        functools.partial(forward_body, first, pieces),
        [longs, where, rows_in, *[piece.array for piece in pieces]],
        through,
        [rows] + blocks,
        out_specs,
        out_shape,
        (total // LONG,),
        "forward_group",
        (8e9, 12e6, 4e6) if first else (0, 0, 0),
        scalars=2,
        scratch=[pltpu.VMEM((PLANE_END[0], GROUP), BF16)],
    )


def attend_back_rows(query, key, value, extra, attended, grad, grad_query, grad_key, grad_value):
    strips = LONG // STRIP
    lane = lax.broadcasted_iota(jnp.int32, (LONG, PAIR), 1)
    row = lax.broadcasted_iota(jnp.int32, (LONG, PAIR), 0)
    row_ids = lax.broadcasted_iota(jnp.int32, (STRIP, STRIP), 0)
    col_ids = lax.broadcasted_iota(jnp.int32, (STRIP, STRIP), 1)
    causal = col_ids >= row_ids
    early = jnp.where((lane == 6) & (row < SHORT), far_below, 0.0)
    v_tail = jnp.where(lane < 3, 1.0, 0.0).astype(BF16)
    heads, pairs = [], query.shape[1] // PAIR
    for pair in range(pairs):
        cols = slice(pair * PAIR, (pair + 1) * PAIR)
        q_all, k_all, v_all, g_all, x_all = (ref[:, cols] for ref in (query, key, value, grad, extra))
        product = g_all.astype(F32) * attended[:, cols].astype(F32)
        zero = jnp.zeros_like(q_all)
        v_wide = jnp.concatenate([v_all, v_tail], 1)
        turned = k_all.astype(F32).T.astype(BF16)
        for side in range(2):
            mine = (lane < HD) if side == 0 else (lane >= HD)
            delta = jnp.sum(jnp.where(mine, product, 0.0), -1, keepdims=True)
            d_tail = pick_lanes(
                jnp.zeros((LONG, PAIR), F32), lane, 0, [part.astype(F32) for part in split_three(-delta)]
            )
            q_head = jnp.where(mine, q_all, zero)
            g_head = jnp.where(mine, g_all, zero)
            ones = jnp.where((lane >= 3 * side) & (lane < 3 * side + 3), 1.0, early).astype(BF16)
            heads.append(
                (
                    q_head,
                    g_head,
                    turned[side * HD : (side + 1) * HD],
                    jnp.concatenate([q_head, x_all], 1),
                    jnp.concatenate([g_head, d_tail.astype(BF16)], 1),
                    jnp.concatenate([k_all, ones], 1),
                    v_wide,
                )
            )

    def products(unit):
        block, head = unit
        lo, hi = block * STRIP, (block + 1) * STRIP
        unused, unused, unused, q_wide, g_wide, k_wide, v_wide = heads[head]
        return dot_nt(k_wide[lo:hi], q_wide[lo:]), dot_nt(v_wide[lo:hi], g_wide[lo:])

    def soften(unit, scores, slope):
        soft = jnp.exp(scores)
        first = jnp.where(causal, soft[:, :STRIP], 0.0)
        soft = first if soft.shape[1] == STRIP else jnp.concatenate([first, soft[:, STRIP:]], 1)
        return soft.astype(BF16), (soft * slope).astype(BF16)

    query_sum = {}

    def gradients(unit, soft, scores):
        block, head = unit
        lo, hi = block * STRIP, (block + 1) * STRIP
        q_head, g_head, k_turned, *unused = heads[head]
        part = dot_nn(k_turned[:, lo:hi], scores)
        for later in range(block, strips):
            piece = part[:, (later - block) * STRIP : (later - block + 1) * STRIP]
            at = (later, head)
            query_sum[at] = query_sum[at] + piece if at in query_sum else piece
        return dot_nn(soft, g_head[lo:]), dot_nn(scores, q_head[lo:])

    units = [(block, head) for block in range(strips) for head in range(len(heads))]
    results = pipeline(units, products, soften, gradients)
    for block in range(strips):
        rows = slice(block * STRIP, (block + 1) * STRIP)
        for pair in range(pairs):
            cols = slice(pair * PAIR, (pair + 1) * PAIR)
            (value_a, key_a), (value_b, key_b) = results[(block, 2 * pair)], results[(block, 2 * pair + 1)]
            grad_value[rows, cols] = (value_a + value_b).astype(BF16)
            grad_key[rows, cols] = (key_a + key_b).astype(BF16)
            two = jnp.concatenate([query_sum[(block, 2 * pair + side)] for side in range(2)], 0)
            grad_query[rows, cols] = (two * (1.0 / math.sqrt(HD))).T.astype(BF16)


def backward_body(steps, where, query, key, value, extra, attended, grad, hidden, late, *refs):
    grad_query, grad_key, grad_value, keep, send, total, rows = refs
    step = pl.program_id(0)
    attend_back_rows(query, key, value, extra, attended, grad, grad_query, grad_key, grad_value)
    three = jnp.concatenate([grad_query[...], grad_key[...], grad_value[...]], 1)
    now = dot_tn(hidden[...], three)

    @pl.when(step == 0)
    def _():
        total[...] = now

    @pl.when(step > 0)
    def _():
        total[...] = total[...] + now

    @pl.when(step == steps - 1)
    def _():
        for part, at in enumerate((ROW_QUERY, ROW_KEY, ROW_VALUE)):
            rows[at : at + D, :] = total[:, part * GROUP : (part + 1) * GROUP].astype(BF16)
        rows[ROW_OUT:, :] = late[...]
        emit_blocks(rows, 0, 0, where, keep, send)


def backward_group(group, where, query, key, value, extra, attended, grad, hidden, late, through):
    total = query.shape[0]
    steps = total // LONG
    part = pl.BlockSpec((LONG, GROUP), lambda s, *refs: (s, 0))
    block = (HALF, BLOCK, GROUP)
    return call_kernel(
        functools.partial(backward_body, steps),
        [where, query, key, value, extra, attended, grad, hidden, late],
        through,
        [part] * 5
        + [
            pl.BlockSpec((LONG, GROUP), lambda s, *refs: (s, group)),
            pl.BlockSpec((LONG, D), lambda s, *refs: (s, 0)),
            pl.BlockSpec((late.shape[0], GROUP), lambda s, *refs: (0, group), pipeline_mode=pl.Buffered(1)),
        ],
        [part] * 3 + [whole(block)] * 2,
        [jax.ShapeDtypeStruct((total, GROUP), BF16)] * 3 + [jax.ShapeDtypeStruct(block, BF16)] * 2,
        (steps,),
        "backward_group",
        (14e9, 16e6, 4e6),
        scratch=[
            pltpu.VMEM((D, 3 * GROUP), F32),
            pltpu.VMEM((ROW_OUT + late.shape[0], GROUP), BF16),
        ],
    )


MID_ROWS = 512
HALF_ROWS = 256
CHUNKS = FF // D
TANH_SCALE = math.sqrt(2.0 / math.pi)


def spread_matrix(size):
    quarter = size // CHUNKS
    to = lax.broadcasted_iota(jnp.int32, (size, size), 0)
    source = lax.broadcasted_iota(jnp.int32, (size, size), 1)
    return (source == CHUNKS * (to % quarter) + to // quarter).astype(BF16)


def interleave(parts):
    started, live = 0, []
    while started < len(parts) or live:
        if started < len(parts):
            live.append(parts[started])
            started += 1
        live = [part for part in live if next(part, True) is None]


def middle_body(steps, pieces, where, tok, grad_out, hidden_a, *refs):
    att_refs, wo_refs, refs = refs[:GROUPS], refs[GROUPS : 2 * GROUPS], refs[2 * GROUPS :]
    sources, refs = refs[: len(pieces)], refs[len(pieces) :]
    (outputs, grad_middle_ref, grad_za_ref, grad_attended, hid_f_ref, chunks_ref, grad_f_ref) = refs[:7]
    (grad_zf_ref, grad_a_ref, d_vec, gate_copy, weights, wide, slope, s_vec) = refs[7:]
    step = pl.program_id(0)
    base = ROW_OUT

    @pl.when(step == 0)
    def _():
        weights[...] = jnp.zeros_like(weights)
        for group in range(GROUPS):
            weights[: PLANE_END[0] - ROW_OUT, group * GROUP : (group + 1) * GROUP] = wo_refs[group][...]
        for piece, source in zip(pieces, sources):
            place_piece(weights, base, where, piece, source, False)
        shuffle = spread_matrix(256)
        for block in range(FF // 256):
            at = ROW_IN - base + block * 256
            part = dot_nn(shuffle, weights[at : at + 256, :]).astype(BF16)
            for chunk in range(CHUNKS):
                wide[chunk, block * 64 : (block + 1) * 64, :] = part[chunk * 64 : (chunk + 1) * 64]
        gate_copy[...] = weights[ROW_GATE_A - base : ROW_GATE_A - base + D, :]
        s_vec[...] = jnp.zeros_like(s_vec)

    w_out = weights.at[ROW_OUT - base : ROW_OUT - base + D]
    gate_attn = weights.at[ROW_GATE_A - base : ROW_GATE_A - base + D]
    gate_ffn = weights.at[ROW_GATE_F - base : ROW_GATE_F - base + D]
    w_down = weights.at[ROW_DOWN - base : ROW_DOWN - base + FF]
    vecs = weights[ROW_VEC - base : ROW_VEC - base + VEC_ROWS, :].astype(F32)
    chunks = [slice(chunk * D, (chunk + 1) * D) for chunk in range(CHUNKS)]

    def part(here):
        hid_a = hidden_a[here, :]
        att = jnp.concatenate([ref[here, :] for ref in att_refs], 1)
        grad = grad_out[here, :].astype(F32)
        branch_a = dot_nn(att, w_out[...])
        gate_a = dot_nn(hid_a, gate_attn[...])
        yield
        branch_a = branch_a + vecs[2:3]
        gate_a = sigmoid(gate_a + vecs[3:4])
        middle = tok[here, :].astype(F32) + gate_a * branch_a
        normed, inv_std = layer_stats(middle)
        hid_f = (normed * vecs[4:5] + vecs[5:6]).astype(BF16)
        hid_f_ref[here, :] = hid_f
        yield
        gate_f = dot_nn(hid_f, gate_ffn[...])
        pre = dot_nn(hid_f, wide[0])
        yield
        branch_f = vecs[6:7]
        for chunk, cols in enumerate(chunks):
            pre = pre + vecs[8 + chunk : 9 + chunk]
            square = pre * pre
            bend = jnp.tanh(pre * (TANH_SCALE + (TANH_SCALE * 0.044715) * square))
            half = 0.5 * (1.0 + bend)
            active = (pre * half).astype(BF16)
            slope[here, cols] = half + (0.5 * pre) * (1.0 - bend * bend) * (
                TANH_SCALE + (3.0 * 0.044715 * TANH_SCALE) * square
            )
            chunks_ref[chunk, here, :] = active
            yield
            if chunk + 1 < CHUNKS:
                pre = dot_nn(hid_f, wide[chunk + 1])
            branch_f = branch_f + dot_nn(active, w_down[cols, :])
            yield
        gate_f = sigmoid(gate_f + vecs[7:8])
        outputs[here, :] = (middle + gate_f * branch_f).astype(BF16)
        grad_branch_f = (grad * gate_f).astype(BF16)
        grad_zf = (grad * branch_f * gate_f * (1.0 - gate_f)).astype(BF16)
        grad_f_ref[here, :] = grad_branch_f
        grad_zf_ref[here, :] = grad_zf
        s_vec[6] += fold_rows(grad_branch_f.astype(F32))
        s_vec[7] += fold_rows(grad_zf.astype(F32))
        yield
        grad_hidden = dot_nt(grad_zf, gate_ffn[...])
        grad_active = dot_nt(grad_branch_f, w_down[chunks[0], :])
        yield
        for chunk, cols in enumerate(chunks):
            grad_pre = (grad_active * slope[here, cols]).astype(BF16)
            chunks_ref[CHUNKS + chunk, here, :] = grad_pre
            s_vec[8 + chunk] += fold_rows(grad_pre.astype(F32))
            yield
            if chunk + 1 < CHUNKS:
                grad_active = dot_nt(grad_branch_f, w_down[chunks[chunk + 1], :])
            grad_hidden = grad_hidden + dot_nt(grad_pre, wide[chunk])
            yield
        s_vec[4] += fold_rows(grad_hidden * normed)
        s_vec[5] += fold_rows(grad_hidden)
        grad_middle = grad + norm_back(grad_hidden * vecs[4:5], normed, inv_std)
        grad_middle_ref[here, :] = grad_middle
        grad_branch_a = (grad_middle * gate_a).astype(BF16)
        grad_za = (grad_middle * branch_a * gate_a * (1.0 - gate_a)).astype(BF16)
        grad_za_ref[here, :] = grad_za
        grad_a_ref[here, :] = grad_branch_a
        s_vec[2] += fold_rows(grad_branch_a.astype(F32))
        s_vec[3] += fold_rows(grad_za.astype(F32))
        yield
        grad_attended[here, :] = dot_nt(grad_branch_a, w_out[...]).astype(BF16)
        yield

    interleave([part(slice(at, at + HALF_ROWS)) for at in range(0, MID_ROWS, HALF_ROWS)])

    @pl.when(step == steps - 1)
    def _():
        d_vec[...] = jnp.sum(s_vec[...], 1).astype(BF16)


def middle_part(where, tokens, grad_out, hidden_a, attended, w_outs, pieces):
    total = tokens.shape[0]
    steps = total // MID_ROWS
    rows_at = lambda width: pl.BlockSpec((MID_ROWS, width), lambda i, *refs: (i, 0))
    shape = lambda width, kind=BF16: jax.ShapeDtypeStruct((total, width), kind)
    results, unused = call_kernel(
        functools.partial(middle_body, steps, pieces),
        [where, tokens, grad_out, hidden_a, *attended, *w_outs, *[piece.array for piece in pieces]],
        [],
        [rows_at(D)] * 3
        + [rows_at(GROUP)] * GROUPS
        + [whole(w_outs[0].shape)] * GROUPS
        + [whole(piece.array.shape) for piece in pieces],
        [rows_at(D)] * 5
        + [pl.BlockSpec((2 * CHUNKS, MID_ROWS, D), lambda i, *refs: (0, i, 0))]
        + [rows_at(D)] * 3
        + [whole((VEC_ROWS, D)), whole((D, D))],
        [shape(D), shape(D, F32), shape(D), shape(D), shape(D)]
        + [jax.ShapeDtypeStruct((2 * CHUNKS, total, D), BF16)]
        + [shape(D)] * 3
        + [jax.ShapeDtypeStruct((VEC_ROWS, D), BF16), jax.ShapeDtypeStruct((D, D), BF16)],
        (steps,),
        "middle_part",
        (24e9, 50e6, 4e6),
        scratch=[
            pltpu.VMEM((ALL_ROWS - ROW_OUT, D), BF16),
            pltpu.VMEM((CHUNKS, D, D), BF16),
            pltpu.VMEM((MID_ROWS, FF), F32),
            pltpu.VMEM((VEC_ROWS, 8, D), F32),
        ],
    )
    return results


PLANE_OUT = [jax.ShapeDtypeStruct((HALF, BLOCK, D), BF16)] * 2
PLANE_SPEC = [whole((HALF, BLOCK, D))] * 2


def ffn_body(where, chunk, grad_f, hidden_f, d_vec, keep_three, send_three, keep_two, send_two, carry, rows, wide):
    step = pl.program_id(0)

    @pl.when(step < CHUNKS)
    def _():
        at = pl.multiple_of(ROW_DOWN - ROW_IN + step * D, D)
        rows[pl.ds(at, D), :] = dot_tn(chunk[...], grad_f[...]).astype(BF16)

    @pl.when(step >= CHUNKS)
    def _():
        wide[step - CHUNKS] = dot_tn(hidden_f[...], chunk[...]).astype(BF16)

    @pl.when(step == CHUNKS - 1)
    def _():
        rows[ROW_VEC - ROW_IN :, :] = d_vec[...]
        emit_blocks(rows, ROW_IN, 3, where, keep_three, send_three)

    @pl.when(step == 2 * CHUNKS - 1)
    def _():
        shuffle = spread_matrix(256)

        @pl.loop(0, FF // 256)
        def _(block):
            quarter = pl.ds(pl.multiple_of(block * 64, 64), 64)
            parts = [wide[chunk, quarter, :] for chunk in range(CHUNKS)]
            to = pl.ds(pl.multiple_of(block * 256, 256), 256)
            rows[to, :] = dot_tn(shuffle, jnp.concatenate(parts, 0)).astype(BF16)

        emit_blocks(rows, ROW_IN, 2, where, keep_two, send_two)
        carry[...] = rows[: PLANE_END[1] - ROW_IN, :]


def ffn_gradient(where, chunks, grad_f, hidden_f, d_vec):
    total = chunks.shape[1]
    carry = PLANE_END[1] - ROW_IN
    results, unused = call_kernel(
        ffn_body,
        [where, chunks, grad_f, hidden_f, d_vec],
        [],
        [
            pl.BlockSpec((pl.Squeezed(), total, D), lambda i, *refs: (i, 0, 0)),
            whole((total, D)),
            whole((total, D)),
            whole((VEC_ROWS, D)),
        ],
        PLANE_SPEC * 2 + [whole((carry, D))],
        PLANE_OUT * 2 + [jax.ShapeDtypeStruct((carry, D), BF16)],
        (2 * CHUNKS,),
        "ffn_gradient",
        (8.6e9, 24e6, 0),
        scratch=[
            pltpu.VMEM((ALL_ROWS - ROW_IN, D), BF16),
            pltpu.VMEM((CHUNKS, D, D), BF16),
        ],
    )
    return results


def gates_body(where, *refs):
    att_refs, refs = refs[:GROUPS], refs[GROUPS:]
    hidden_a, hidden_f, grad_a, grad_za, grad_zf, late, keep, send, carry, rows = refs
    att = jnp.concatenate([ref[...] for ref in att_refs], 1)
    rows[:D, :] = dot_tn(att, grad_a[...]).astype(BF16)
    rows[D : 2 * D, :] = dot_tn(hidden_a[...], grad_za[...]).astype(BF16)
    rows[2 * D : 3 * D, :] = dot_tn(hidden_f[...], grad_zf[...]).astype(BF16)
    rows[3 * D :, :] = late[...]
    emit_blocks(rows, ROW_OUT, 1, where, keep, send)
    carry[...] = rows[: PLANE_END[0] - ROW_OUT, :]


def gates_gradient(where, attended, hidden_a, hidden_f, grad_a, grad_za, grad_zf, late, through):
    total = hidden_a.shape[0]
    carry = PLANE_END[0] - ROW_OUT
    return call_kernel(
        gates_body,
        [where, *attended, hidden_a, hidden_f, grad_a, grad_za, grad_zf, late],
        through,
        [whole((total, GROUP))] * GROUPS + [whole((total, D))] * 5 + [whole(late.shape)],
        PLANE_SPEC + [whole((carry, D))],
        PLANE_OUT + [jax.ShapeDtypeStruct((carry, D), BF16)],
        (1,),
        "gates_gradient",
        (3.2e9, 14e6, 0),
        scratch=[pltpu.VMEM((3 * D + late.shape[0], D), BF16)],
    )


LAST_ROWS = 512


def last_body(steps, tok, grad_middle, grad_za, *refs):
    grads, refs = refs[: 3 * GROUPS], refs[3 * GROUPS :]
    w_three, refs = refs[:GROUPS], refs[GROUPS:]
    gate_attn, vec, input_grad, d_vec, factors, s_vec = refs
    step = pl.program_id(0)

    @pl.when(step == 0)
    def _():
        s_vec[...] = jnp.zeros_like(s_vec)
        for group in range(GROUPS):
            factors[:, group * GROUP : (group + 1) * GROUP] = w_three[group][...]

    vecs = vec[...].astype(F32)
    normed, inv_std = layer_stats(tok[...].astype(F32))
    grad_hidden = dot_nt(grad_za[...], gate_attn[...])
    for part, at in enumerate((ROW_QUERY, ROW_KEY, ROW_VALUE)):
        grad = jnp.concatenate([grads[3 * group + part][...] for group in range(GROUPS)], 1)
        grad_hidden += dot_nt(grad, factors[at : at + D, :])
    s_vec[0] += fold_rows(grad_hidden * normed)
    s_vec[1] += fold_rows(grad_hidden)
    input_grad[...] = (grad_middle[...] + norm_back(grad_hidden * vecs[0:1], normed, inv_std)).astype(BF16)

    @pl.when(step == steps - 1)
    def _():
        d_vec[...] = jnp.sum(s_vec[...], 1)


def last_part(tokens, grad_middle, grad_za, grads, w_three, gate_attn, vec, through):
    total = tokens.shape[0]
    steps = total // LAST_ROWS
    rows_at = lambda width: pl.BlockSpec((LAST_ROWS, width), lambda i, *refs: (i, 0))
    return call_kernel(
        functools.partial(last_body, steps),
        [tokens, grad_middle, grad_za, *grads, *w_three, gate_attn, vec],
        through,
        [rows_at(D)] * 3
        + [rows_at(GROUP)] * (3 * GROUPS)
        + [whole((ROW_OUT, GROUP))] * GROUPS
        + [whole((D, D)), whole((VEC_ROWS, D))],
        [rows_at(D), whole((VEC_ROWS, D))],
        [jax.ShapeDtypeStruct((total, D), BF16), jax.ShapeDtypeStruct((VEC_ROWS, D), F32)],
        (steps,),
        "last_part",
        (4.3e9, 20e6, 0),
        scalars=0,
        scratch=[pltpu.VMEM((ROW_OUT, D), BF16), pltpu.VMEM((VEC_ROWS, 8, D), F32)],
    )


def local_part(where, longs, tokens, out_grad, first_pieces, middle_pieces, before, later, collect):
    subs, length, unused = tokens.shape
    rows = tokens.reshape(subs * length, D)
    grads_in = out_grad.reshape(subs * length, D)
    (*kept, hidden_a, vec), passed = forward_group(0, longs, where, rows, first_pieces, before("forward0"))
    later("forward0", passed)
    second, passed = forward_group(1, longs, where, hidden_a, first_pieces, before("forward1"))
    later("forward1", passed)
    groups = [kept, second]
    attended = [group[3] for group in groups]
    (outputs, grad_middle, grad_za, grad_attended, hidden_f, chunks, grad_f, grad_zf, grad_a, d_vec, gate_attn) = (
        middle_part(where, rows, grads_in, hidden_a, attended, [group[6] for group in groups], middle_pieces())
    )
    keep, send, *plane, carry = ffn_gradient(where, chunks, grad_f, hidden_f, d_vec)
    collect(3, keep, send)
    collect(2, *plane)
    (*plane, carry), passed = gates_gradient(
        where, attended, hidden_a, hidden_f, grad_a, grad_za, grad_zf, carry, before("gates")
    )
    later("gates", passed)
    collect(1, *plane)
    grads = []
    for group, (query, key, value, att, extra, *unused_two) in enumerate(groups):
        (*three, keep, send), passed = backward_group(
            group, where, query, key, value, extra, att, grad_attended, hidden_a, carry, before(f"back{group}")
        )
        later(f"back{group}", passed)
        grads += three
        collect(("first", group), keep, send)
    w_three = [group[5] for group in groups]
    (input_grad, d_vec), passed = last_part(
        rows, grad_middle, grad_za, grads, w_three, gate_attn, vec, before("last")
    )
    later("last", passed)
    return outputs.reshape(tokens.shape), input_grad.reshape(tokens.shape), d_vec


def own_block(params, start, rows):
    share = params.shape[0]
    room = jnp.pad(params, (TILE, rows * D - share))
    return lax.dynamic_slice(room, (TILE - start % TILE,), (rows * D,)).reshape(rows, D).astype(BF16)


def move(axis, count, step):
    perm = [(i, step(i)) for i in range(count) if step(i) is not None]
    return lambda value: lax.ppermute(value, axis, perm)


def on_slice(tokens, out_grad, long_count, params):
    z, x, y, c = (lax.axis_index(axis) for axis in ("z", "x", "y", "c"))
    me = ((z * 2 + x) * 2 + y) * 2 + c
    share = params.shape[0]
    block = own_block(params, me * share, BLOCK)
    odd = z % 2 == 1
    ends = (z == 0) | (z == 3)
    swap_c = move("c", 2, lambda i: 1 - i)
    swap_x = move("x", 2, lambda i: 1 - i)
    swap_y = move("y", 2, lambda i: 1 - i)
    swap_xy = move(("x", "y"), 4, lambda i: 3 - i)
    z_one = move("z", 4, lambda i: i ^ 1)
    z_two = move("z", 4, lambda i: i ^ 2)
    z_ends = move("z", 4, lambda i: {0: 2, 3: 1}.get(i))
    z_mid = move("z", 4, lambda i: {1: 2, 2: 1}.get(i))
    z_out = move("z", 4, lambda i: {1: 0, 2: 3}.get(i))

    inside = z < 4
    vec = block[VEC_AT : VEC_AT + VEC_ROWS]
    mine = jnp.concatenate([block, jnp.where(me == SHARES - 1, vec, jnp.zeros_like(vec))], 0)
    held = jnp.where(ends, mine, z_ends(mine))
    out_first, got_mid = z_out(block), z_mid(block)
    got = z_one(jnp.concatenate([held, jnp.where(inside, got_mid, out_first)], 0))
    other, out_second = got[: BLOCK + VEC_ROWS], got[BLOCK + VEC_ROWS :]
    vec = jnp.where(odd, held, other)[BLOCK:]
    first = jnp.concatenate([jnp.where(z == 2, held, other)[:BLOCK], vec], 0)[None]
    one = jnp.where(z == 0, out_first, jnp.where(z == 1, held[:BLOCK], jnp.where(z == 2, got_mid, out_second)))
    two = jnp.where(z == 0, out_second, jnp.where(z == 1, got_mid, jnp.where(z == 2, other[:BLOCK], out_first)))
    both = jnp.stack([one, two])

    def in_plane(parts, planes):
        near = jnp.concatenate(parts, 0)
        blocks = [(plane, spot) for spot in range(HALF) for plane in planes]
        return [Piece(near, blocks, False, 0), Piece(swap_c(near), blocks, True, 0)]

    own = block[None]
    pieces = in_plane([own, swap_y(own), swap_x(own), swap_xy(own)], ((0,),))
    pieces += in_plane([first, swap_y(first), swap_x(first), swap_xy(first)], ((4,),))
    around = {"both": [swap_y(both), swap_x(both), swap_xy(both)]}
    top = {"both": both[:, :TILE_ROWS]}

    def middle_pieces():
        mine = jnp.concatenate([top["both"], both[:, TILE_ROWS:]], 1)
        return pieces + in_plane([mine] + around["both"], ((5,), (6,)))

    early, late = ("first", 0), ("first", 1)
    arrived, at_chip, held = {}, {}, {}
    z_up = move("z", 4, lambda i: {0: 2, 1: 3}.get(i))
    z_down = move("z", 4, lambda i: {2: 0, 3: 1}.get(i))

    def collect(plane, keep, send):
        arrived[plane] = [keep, swap_c(send)]

    def send_around(name, planes, first=None):
        part = []
        for spot in range(HALF):
            sides = [[arrived[plane][side][spot].astype(F32) for plane in planes] for side in range(2)]
            keep, got = (jnp.concatenate(side, 1) for side in sides)
            if first is not None:
                keep = jnp.where(inside, keep, first[:, : keep.shape[1]])
            part.append((keep + got).astype(BF16))
        at_chip[name] = part[0]
        around[name] = (swap_y(part[1]), swap_x(part[2]), swap_xy(part[3]))

    def plane_sum(name):
        total = at_chip[name].astype(F32)
        for got in around[name]:
            total = total + got.astype(F32)
        return total

    def before(name):
        if name == "forward0":
            return []
        if name == "forward1":
            return [top["both"]]
        if name == "gates":
            return [arrived[2][0], arrived[3][0]]
        if name == "back0":
            send_around("upper", (2, 3))
            return [at_chip["upper"]]
        if name == "back1":
            held["upper"] = plane_sum("upper")
            held["up"] = z_up(held["upper"].astype(BF16))
            send_around("lower", (1, early), held["upper"])
            return [held["upper"], at_chip["lower"]]
        if name == "last":
            held["lower"] = plane_sum("lower")
            held["down"] = z_down(held["lower"].astype(BF16))
            send_around("late", (late,), held["lower"])
            upper = jnp.where(inside, held["upper"][:, : D + GROUP], held["lower"])
            upper = jnp.concatenate([upper, held["upper"][:, D + GROUP :]], 1) + held["up"].astype(F32)
            two, three = upper[:, :D], upper[:, D:]
            held["give"] = jnp.where(z == 2, three, two).astype(BF16)
            held["mine"] = jnp.where(z == 2, two, three)
            return [held["give"], held["mine"], held["lower"], at_chip["late"]]
        return []

    def later(name, passed):
        if name == "forward1":
            top["both"] = passed[0]
        if name == "gates":
            arrived[2][0], arrived[3][0] = passed
        if name == "back0":
            at_chip["upper"] = passed[0]
        if name == "back1":
            held["upper"], at_chip["lower"] = passed
        if name == "last":
            held["give"], held["mine"], held["lower"], at_chip["late"] = passed

    planes = [jnp.where(z == 0, 3, 0), jnp.where(z == 1, 3, 1), jnp.where(z == 2, 3, 2)]
    where = jnp.stack([z, x, y, c, *planes]).astype(jnp.int32)
    outputs, input_grad, d_vec = local_part(
        where,
        long_count.reshape(-1),
        tokens,
        out_grad,
        pieces,
        middle_pieces,
        before,
        later,
        collect,
    )
    low = plane_sum("late")
    lower = jnp.where(inside, held["lower"], jnp.concatenate([low] * 3, 1)) + held["down"].astype(F32)
    one, zero = lower[:, :D], jnp.concatenate([lower[:, D:]] * 2, 1)
    give = jnp.where(z == 0, one.astype(BF16), jnp.where(z == 1, zero.astype(BF16), held["give"]))
    given = z_one(give).astype(F32)
    total = jnp.where(z == 0, zero, jnp.where(z == 1, one, held["mine"])) + given
    gains = jnp.where(inside, d_vec[:2], jnp.concatenate([low[:2]] * 2, 1))
    gains = gains + swap_c(gains)
    gains = (gains + swap_x(gains) + swap_y(gains) + swap_xy(gains)).reshape(2 * GROUPS, GROUP)
    lines = jnp.pad(gains.astype(BF16), ((0, TILE_ROWS - 2 * GROUPS), (0, 0)))
    message = jnp.concatenate([low.astype(BF16), lines], 0)
    for step in ({3: 0, 0: 3}, {2: 0, 1: 3}, {1: 0, 2: 3}):
        got = move("z", 4, step.get)(message).astype(F32)
        low = low + got[:BLOCK]
        gains = gains + got[BLOCK : BLOCK + 2 * GROUPS]
    total = jnp.where(z == 0, jnp.concatenate([total[:, :GROUP], low], 1), total)
    gains = jnp.where(me == SHARES - 1, gains.reshape(2, D), jnp.zeros((2, D), F32))
    total = total + jnp.pad(gains, ((VEC_AT, BLOCK - VEC_AT - 2), (0, 0)))
    param_grad = lax.dynamic_slice(total.reshape(-1), ((me * share) % TILE,), (share,))
    return (outputs, input_grad, param_grad)


def on_any(axes, count, tokens, out_grad, long_count, params):
    share = params.shape[0]
    me = lax.axis_index(axes)
    starts = [index * share // TILE * TILE_ROWS for index in range(count)]
    rows = max(-(-((index + 1) * share) // TILE) * TILE_ROWS - starts[index] for index in range(count))
    gathered = lax.all_gather(own_block(params, me * share, rows), axes, axis=0)
    merged = jnp.zeros((starts[-1] + rows, D), BF16)
    for index in range(count):
        merged = merged.at[starts[index] : starts[index] + rows].add(gathered[index])
    merged = merged[:ALL_ROWS]
    near, far = [], []
    for plane in range(PLANES):
        blocks = []
        for index in range(plane * IN_PLANE, (plane + 1) * IN_PLANE):
            end = STARTS[index + 1] if index + 1 < SHARES else ALL_ROWS
            piece = merged[STARTS[index] : end]
            blocks.append(jnp.pad(piece, ((0, BLOCK - piece.shape[0]), (0, 0))))
        spots = [(plane, spot) for spot in range(HALF)]
        near.append(Piece(jnp.stack(blocks[0::2]), spots, False, 0))
        far.append(Piece(jnp.stack(blocks[1::2]), spots, True, 0))
    vec = merged[ROW_VEC : ROW_VEC + VEC_ROWS]
    first_pieces = []
    for piece in (near[0], far[0]):
        lines = jnp.zeros((HALF, VEC_ROWS, D), BF16)
        if piece is near[0]:
            lines = lines.at[0].set(vec)
        first_pieces.append(Piece(jnp.concatenate([piece.array, lines], 1), piece.blocks, piece.other, 0))
    by_share = [None] * SHARES

    halves = []

    def collect(plane, keep, send):
        if isinstance(plane, tuple):
            halves.append((keep, send))
            if len(halves) < GROUPS:
                return
            keep, send = (jnp.concatenate([half[side] for half in halves], 2) for side in range(2))
            plane = 0
        for spot in range(HALF):
            by_share[plane * IN_PLANE + 2 * spot] = keep[spot]
            by_share[plane * IN_PLANE + 2 * spot + 1] = send[spot]

    outputs, input_grad, d_vec = local_part(
        jnp.zeros((7,), jnp.int32),
        long_count.reshape(-1),
        tokens,
        out_grad,
        first_pieces,
        lambda: near[1:] + far[1:],
        lambda name: [],
        lambda name, passed: None,
        collect,
    )
    ends = STARTS[1:] + [ALL_ROWS]
    gradient = jnp.concatenate([part[: ends[i] - STARTS[i]] for i, part in enumerate(by_share)], 0)
    gradient = gradient.at[ROW_VEC : ROW_VEC + VEC_ROWS].add(d_vec.astype(BF16))
    gradient = jnp.pad(gradient, ((0, max(0, starts[-1] + rows - ALL_ROWS)), (0, 0)))
    spread = jnp.stack([gradient[start : start + rows] for start in starts])
    summed = lax.psum_scatter(spread, axes, scatter_dimension=0)
    param_grad = lax.dynamic_slice(summed.astype(F32).reshape(-1), ((me * share) % TILE,), (share,))
    return (outputs, input_grad, param_grad)


def solution(mesh):
    axes = ("wide", "narrow")
    count = math.prod(mesh.shape[axis] for axis in axes)
    step = functools.partial(on_any, axes, count)
    if mesh.shape["wide"] == 8 and mesh.shape["narrow"] == 4:
        axes = ("z", "x", "y", "c")
        mesh = Mesh(mesh.devices.reshape(4, 2, 2, 2), axes)
        step = on_slice
    return jax.shard_map(
        step,
        mesh=mesh,
        in_specs=(P(None, axes, None), P(None, axes, None), P(None, axes), P(axes)),
        out_specs=(P(None, axes, None), P(None, axes, None), P(axes)),
        check_vma=False,
    )
```

profile of v0, /device:TPU:0, one launch (start us, length us, event | category | flops | bytes accessed | tf_op | source)
XLA Modules:
  0.0 283.0 jit_solution(14838465749766205599)
XLA Ops:
  4.1 9.4 %collective-permute-start.4 = (bf16[256,512]{1,0:T(8,128)(2,1)S(1)}, bf16[256,512]{1,0:T(8,128)(2,1)S(1)}, u32[]{:S(2)}, u32[]{:S(2)}) collective-permute-start(bf16[256,512]{1,0:T(8,128)(2,1)S(1)} %constant_dynamic-update-slice_fusion.4), channel_id=1, source_target_pairs={{0,16},{24,8},{1,17},{25,9},{2,18},{26,10},{3,19},{27,11},{4,20},{... | collective-permute-start | bytes 786440 | tf_op jit(solution)/shard_map/ppermute | solution.py:808
  13.6 5.2 %collective-permute-done.4 = bf16[256,512]{1,0:T(8,128)(2,1)S(1)} collective-permute-done((bf16[256,512]{1,0:T(8,128)(2,1)S(1)}, bf16[256,512]{1,0:T(8,128)(2,1)S(1)}, u32[]{:S(2)}, u32[]{:S(2)}) %collective-permute-start.4) | collective-permute-done | bytes 262176 | tf_op jit(solution)/shard_map/ppermute | solution.py:808
  18.9 4.6 %collective-permute-start.7 = (bf16[496,512]{1,0:T(8,128)(2,1)S(1)}, bf16[496,512]{1,0:T(8,128)(2,1)S(1)}, u32[]{:S(2)}, u32[]{:S(2)}) collective-permute-start(bf16[496,512]{1,0:T(8,128)(2,1)S(1)} %pad_maximum_fusion.3), channel_id=1, source_target_pairs={{0,8},{8,0},{16,24},{24,16},{1,9},{9,1},{17,25},{25,17},{2,10},{10... | collective-permute-start | bytes 1523720 | tf_op jit(solution)/shard_map/ppermute | solution.py:808
  26.8 6.3 %collective-permute-done.7 = bf16[496,512]{1,0:T(8,128)(2,1)S(1)} collective-permute-done((bf16[496,512]{1,0:T(8,128)(2,1)S(1)}, bf16[496,512]{1,0:T(8,128)(2,1)S(1)}, u32[]{:S(2)}, u32[]{:S(2)}) %collective-permute-start.7) | collective-permute-done | bytes 507936 | tf_op jit(solution)/shard_map/ppermute | solution.py:808
  33.2 2.5 collective-permute-start.10
  36.8 2.5 collective-permute-start.2
  39.4 4.2 %collective-permute-done.10 = bf16[1,256,512]{2,1,0:T(8,128)(2,1)S(1)} collective-permute-done((bf16[1,256,512]{2,1,0:T(8,128)(2,1)S(1)}, bf16[1,256,512]{2,1,0:T(8,128)(2,1)S(1)}, u32[]{:S(2)}, u32[]{:S(2)}) %collective-permute-start.10) | collective-permute-done | bytes 262176 | tf_op jit(solution)/shard_map/ppermute | solution.py:808
  43.5 4.4 %collective-permute-done.9 = bf16[1,256,512]{2,1,0:T(8,128)(2,1)S(1)} collective-permute-done((bf16[1,256,512]{2,1,0:T(8,128)(2,1)S(1)}, bf16[1,256,512]{2,1,0:T(8,128)(2,1)S(1)}, u32[]{:S(2)}, u32[]{:S(2)}) %collective-permute-start.9) | collective-permute-done | bytes 262176 | tf_op jit(solution)/shard_map/ppermute | solution.py:808
  48.1 2.3 collective-permute-done.2
  56.4 14.4 %forward_group.2 = (bf16[2048,256]{1,0:T(8,128)(2,1)}, bf16[2048,256]{1,0:T(8,128)(2,1)}, bf16[2048,256]{1,0:T(8,128)(2,1)}, bf16[2048,256]{1,0:T(8,128)(2,1)}, ...) custom-call(s32[2]{0:T(128)} %bitcast.121, ...), custom_call_target="tpu_custom_call" | custom-call | flops 8000000000 | bytes 12000000 | tf_op jit(solution)/shard_map/forward_group/pallas_call | solution.py:143
  70.8 12.8 %forward_group.3 = (bf16[2048,256]{1,0:T(8,128)(2,1)}, bf16[2048,256]{1,0:T(8,128)(2,1)}, bf16[2048,256]{1,0:T(8,128)(2,1)}, bf16[2048,256]{1,0:T(8,128)(2,1)}, ...) custom-call(s32[2]{0:T(128)} %bitcast.122, ...), custom_call_target="tpu_custom_call", output_to_operand_aliasing={{7}: (7, {})} | custom-call | tf_op jit(solution)/shard_map/forward_group/pallas_call | solution.py:143
  85.7 4.0 %collective-permute-done.15.refs_13_ = bf16[8,240,512]{2,1,0:T(8,128)(2,1)S(1)} collective-permute-done((bf16[8,240,512]{2,1,0:T(8,128)(2,1)S(1)}, bf16[8,240,512]{2,1,0:T(8,128)(2,1)S(1)}, u32[]{:S(2)}, u32[]{:S(2)}) %collective-permute-start.15) | collective-permute-done | bytes 1966112 | tf_op jit(solution)/shard_map/ppermute | solution.py:808
  91.0 44.4 %middle_part.1 = (bf16[2048,512]{1,0:T(8,128)(2,1)}, f32[2048,512]{1,0:T(8,128)}, bf16[2048,512]{1,0:T(8,128)(2,1)}, bf16[2048,512]{1,0:T(8,128)(2,1)}, bf16[204...) custom-call(s32[7]{0:T(128)} %stack.40.refs_1_.refs_0_, ...), custom_call_target="tpu_custom_call" | custom-call | flops 24000000000 | bytes 50000000 | tf_op jit(solution)/shard_map/middle_part/pallas_call | solution.py:143
  135.4 19.7 %ffn_gradient.1 = (bf16[4,240,512]{2,1,0:T(8,128)(2,1)}, bf16[4,240,512]{2,1,0:T(8,128)(2,1)}, bf16[4,240,512]{2,1,0:T(8,128)(2,1)}, bf16[4,240,512]{2,1,0:T(8,128)(2,1)}, bf16[528,512]{1,0:T(8,128)(2,1)}) custom-call(s32[7]{0:T(128)} %stack.40.refs_1_.refs_0_, bf16[8,2048,512]{2,1,0:T(8,128)(2,1)} %get-tuple-element.77.refs_1_, ...), custom_call_target="tpu_custom_call" | custom-call | flops 8600000512 | bytes 24000000 | tf_op jit(solution)/shard_map/ffn_gradient/pallas_call | solution.py:143
  155.7 10.4 %gates_gradient.1 = (bf16[4,240,512]{2,1,0:T(8,128)(2,1)}, bf16[4,240,512]{2,1,0:T(8,128)(2,1)}, bf16[272,512]{1,0:T(8,128)(2,1)}, bf16[4,240,512]{2,1,0:T(8,128)(2,1)}, bf16[4,240,512]{2,1,0:T(8,128)(2,1)}) custom-call(s32[7]{0:T(128)} %stack.40.refs_1_.refs_0_, ...), custom_call_target="tpu_custom_call", output_to_operand_aliasing={{3}: (9, {}), {4}: (10, {})} | custom-call | flops 3200000000 | bytes 14000000 | tf_op jit(solution)/shard_map/gates_gradient/pallas_call | solution.py:143
  168.5 2.6 collective-permute-start.20
  174.1 21.9 %backward_group.2 = (bf16[2048,256]{1,0:T(8,128)(2,1)}, bf16[2048,256]{1,0:T(8,128)(2,1)}, bf16[2048,256]{1,0:T(8,128)(2,1)}, bf16[4,240,256]{2,1,0:T(8,128)(2,1...) custom-call(s32[7]{0:T(128)} %stack.40.refs_1_.refs_0_, ...), custom_call_target="tpu_custom_call", output_to_operand_aliasing={{5}: (9, {})} | custom-call | flops 14000000000 | bytes 16000000 | tf_op jit(solution)/shard_map/backward_group/pallas_call | solution.py:143
  199.4 6.3 %collective-permute-start.26 = (bf16[240,1024]{1,0:T(8,128)(2,1)}, bf16[240,1024]{1,0:T(8,128)(2,1)S(1)}, u32[]{:S(2)}, u32[]{:S(2)}) collective-permute-start(bf16[240,1024]{1,0:T(8,128)(2,1)} %get-tuple-element.121), channel_id=1, source_target_pairs={{0,16},{8,24},{1,17},{9,25},{2,18},{10,26},{3,19},{11,27},{4,20},{... | collective-permute-start | bytes 1474568 | tf_op jit(solution)/shard_map/ppermute | solution.py:808
  210.5 22.2 %backward_group.3 = (bf16[2048,256]{1,0:T(8,128)(2,1)}, bf16[2048,256]{1,0:T(8,128)(2,1)}, bf16[2048,256]{1,0:T(8,128)(2,1)}, bf16[4,240,256]{2,1,0:T(8,128)(2,1...) custom-call(s32[7]{0:T(128)} %stack.40.refs_1_.refs_0_, ...), custom_call_target="tpu_custom_call", output_to_operand_aliasing={{5}: (9, {}), {6}: (10, {})} | custom-call | flops 14000000000 | bytes 16000000 | tf_op jit(solution)/shard_map/backward_group/pallas_call | solution.py:143
  242.6 11.5 %last_part.1 = (bf16[2048,512]{1,0:T(8,128)(2,1)}, f32[16,512]{1,0:T(8,128)}, bf16[240,512]{1,0:T(8,128)(2,1)}, f32[240,512]{1,0:T(8,128)}, f32[240,768]{1,0:T(8,128)}, /*index=5*/bf16[240,256]{1,0:T(8,128)(2,1)}) custom-call(bf16[2048,512]{1,0:T(8,128)(2,1)} %bitcast.119, ...), custom_call_target="tpu_custom_call", output_to_operand_aliasing={{2}: (13, {}), {3}: (14, {}), {4}: (15, {}), {5}: (16, {})} | custom-call | flops 4300000256 | bytes 20000000 | tf_op jit(solution)/shard_map/last_part/pallas_call | solution.py:143
  257.1 2.5 collective-permute-start.36
  266.3 5.5 %collective-permute-start.37 = (bf16[256,256]{1,0:T(8,128)(2,1)S(1)}, bf16[256,256]{1,0:T(8,128)(2,1)S(1)}, u32[]{:S(2)}, u32[]{:S(2)}) collective-permute-start(bf16[256,256]{1,0:T(8,128)(2,1)S(1)} %fusion.18), channel_id=1, source_target_pairs={{0,24},{24,0},{1,25},{25,1},{2,26},{26,2},{3,27},{27,3},{4,28},{28... | collective-permute-start | bytes 393224 | tf_op jit(solution)/shard_map/ppermute | solution.py:808
  273.3 3.3 %collective-permute-done.39 = bf16[256,256]{1,0:T(8,128)(2,1)S(1)} collective-permute-done((bf16[256,256]{1,0:T(8,128)(2,1)S(1)}, bf16[256,256]{1,0:T(8,128)(2,1)S(1)}, u32[]{:S(2)}, u32[]{:S(2)}) %collective-permute-start.39) | collective-permute-done | bytes 131104 | tf_op jit(solution)/shard_map/ppermute | solution.py:808
  276.8 4.7 %collective-permute-done.32 = bf16[240,512]{1,0:T(8,128)(2,1)S(1)} collective-permute-done((bf16[240,512]{1,0:T(8,128)(2,1)S(1)}, bf16[240,512]{1,0:T(8,128)(2,1)S(1)}, u32[]{:S(2)}, u32[]{:S(2)}) %collective-permute-start.32) | collective-permute-done | bytes 245792 | tf_op jit(solution)/shard_map/ppermute | solution.py:808
  (159 shorter events, 53.9 us)
Async XLA Ops:
  4.1 14.7 %collective-permute-start.4 = (bf16[256,512]{1,0:T(8,128)(2,1)S(1)}, bf16[256,512]{1,0:T(8,128)(2,1)S(1)}, u32[]{:S(2)}, u32[]{:S(2)}) collective-permute-start(bf16[256,512]{1,0:T(8,128)(2,1)S(1)} %constant_dynamic-update-slice_fusion.4), channel_id=1, source_target_pairs={{0,16},{24,8},{1,17},{25,9},{2,18},{26,10},{3,19},{27,11},{4,20},{... | collective-permute-start | bytes 786440 | tf_op jit(solution)/shard_map/ppermute | solution.py:808
  18.9 14.1 %collective-permute-start.7 = (bf16[496,512]{1,0:T(8,128)(2,1)S(1)}, bf16[496,512]{1,0:T(8,128)(2,1)S(1)}, u32[]{:S(2)}, u32[]{:S(2)}) collective-permute-start(bf16[496,512]{1,0:T(8,128)(2,1)S(1)} %pad_maximum_fusion.3), channel_id=1, source_target_pairs={{0,8},{8,0},{16,24},{24,16},{1,9},{9,1},{17,25},{25,17},{2,10},{10... | collective-permute-start | bytes 1523720 | tf_op jit(solution)/shard_map/ppermute | solution.py:808
  23.7 15.6 %collective-permute-start.1 = (bf16[1,240,512]{2,1,0:T(8,128)(2,1)S(1)}, bf16[1,240,512]{2,1,0:T(8,128)(2,1)S(1)}, u32[]{:S(2)}, u32[]{:S(2)}) collective-permute-start(bf16[1,240,512]{2,1,0:T(8,128)(2,1)S(1)} %convert_element_type.310), channel_id=1, source_target_pairs={{0,4},{4,0},{1,5},{5,1},{2,6},{6,2},{3,7},{7,3},{8,12},{12,8},{9,1... | collective-permute-start | bytes 737288 | tf_op jit(solution)/shard_map/ppermute | solution.py:808
  35.7 12.2 %collective-permute-start.9 = (bf16[1,256,512]{2,1,0:T(8,128)(2,1)S(1)}, bf16[1,256,512]{2,1,0:T(8,128)(2,1)S(1)}, u32[]{:S(2)}, u32[]{:S(2)}) collective-permute-start(bf16[1,256,512]{2,1,0:T(8,128)(2,1)S(1)} %maximum_bitcast_fusion), channel_id=1, source_target_pairs={{0,4},{4,0},{1,5},{5,1},{2,6},{6,2},{3,7},{7,3},{8,12},{12,8},{9,1... | collective-permute-start | bytes 786440 | tf_op jit(solution)/shard_map/ppermute | solution.py:808
  36.3 11.6 %collective-permute-start.8 = (bf16[1,256,512]{2,1,0:T(8,128)(2,1)S(1)}, bf16[1,256,512]{2,1,0:T(8,128)(2,1)S(1)}, u32[]{:S(2)}, u32[]{:S(2)}) collective-permute-start(bf16[1,256,512]{2,1,0:T(8,128)(2,1)S(1)} %maximum_bitcast_fusion), channel_id=1, source_target_pairs={{0,2},{2,0},{1,3},{3,1},{4,6},{6,4},{5,7},{7,5},{8,10},{10,8},{9,1... | collective-permute-start | bytes 786440 | tf_op jit(solution)/shard_map/ppermute | solution.py:808
  36.8 13.6 %collective-permute-start.2 = (bf16[1,240,512]{2,1,0:T(8,128)(2,1)S(1)}, bf16[1,240,512]{2,1,0:T(8,128)(2,1)S(1)}, u32[]{:S(2)}, u32[]{:S(2)}) collective-permute-start(bf16[1,240,512]{2,1,0:T(8,128)(2,1)S(1)} %convert_element_type.310), channel_id=1, source_target_pairs={{0,6},{2,4},{4,2},{6,0},{1,7},{3,5},{5,3},{7,1},{8,14},{10,12},{12... | collective-permute-start | bytes 737288 | tf_op jit(solution)/shard_map/ppermute | solution.py:808
  52.2 31.4 %collective-permute-start.12 = (bf16[2,240,512]{2,1,0:T(8,128)(2,1)}, bf16[2,240,512]{2,1,0:T(8,128)(2,1)S(1)}, u32[]{:S(2)}, u32[]{:S(2)}) collective-permute-start(bf16[2,240,512]{2,1,0:T(8,128)(2,1)} %pad_maximum_fusion.2), channel_id=1, source_target_pairs={{0,2},{2,0},{1,3},{3,1},{4,6},{6,4},{5,7},{7,5},{8,10},{10,8},{9,1... | collective-permute-start | bytes 1474568 | tf_op jit(solution)/shard_map/ppermute | solution.py:808
  53.8 29.9 %collective-permute-start.13 = (bf16[2,240,512]{2,1,0:T(8,128)(2,1)}, bf16[2,240,512]{2,1,0:T(8,128)(2,1)}, u32[]{:S(2)}, u32[]{:S(2)}) collective-permute-start(bf16[2,240,512]{2,1,0:T(8,128)(2,1)} %pad_maximum_fusion.2), channel_id=1, source_target_pairs={{0,4},{4,0},{1,5},{5,1},{2,6},{6,2},{3,7},{7,3},{8,12},{12,8},{9,1... | collective-permute-start | bytes 1474568 | tf_op jit(solution)/shard_map/ppermute | solution.py:808
  55.2 28.4 %collective-permute-start.14 = (bf16[2,240,512]{2,1,0:T(8,128)(2,1)}, bf16[2,240,512]{2,1,0:T(8,128)(2,1)}, u32[]{:S(2)}, u32[]{:S(2)}) collective-permute-start(bf16[2,240,512]{2,1,0:T(8,128)(2,1)} %pad_maximum_fusion.2), channel_id=1, source_target_pairs={{0,6},{2,4},{4,2},{6,0},{1,7},{3,5},{5,3},{7,1},{8,14},{10,12},{12... | collective-permute-start | bytes 1474568 | tf_op jit(solution)/shard_map/ppermute | solution.py:808
  155.1 13.1 %collective-permute-start.16 = (bf16[4,240,512]{2,1,0:T(8,128)(2,1)}, bf16[4,240,512]{2,1,0:T(8,128)(2,1)S(1)}, u32[]{:S(2)}, u32[]{:S(2)}) collective-permute-start(bf16[4,240,512]{2,1,0:T(8,128)(2,1)} %get-tuple-element.86), channel_id=1, source_target_pairs={{0,1},{1,0},{2,3},{3,2},{4,5},{5,4},{6,7},{7,6},{8,9},{9,8},{10,11... | collective-permute-start | bytes 2949128 | tf_op jit(solution)/shard_map/ppermute | solution.py:808
  155.4 12.8 %collective-permute-start.17 = (bf16[4,240,512]{2,1,0:T(8,128)(2,1)}, bf16[4,240,512]{2,1,0:T(8,128)(2,1)S(1)}, u32[]{:S(2)}, u32[]{:S(2)}) collective-permute-start(bf16[4,240,512]{2,1,0:T(8,128)(2,1)} %get-tuple-element.87), channel_id=1, source_target_pairs={{0,1},{1,0},{2,3},{3,2},{4,5},{5,4},{6,7},{7,6},{8,9},{9,8},{10,11... | collective-permute-start | bytes 2949128 | tf_op jit(solution)/shard_map/ppermute | solution.py:808
  166.1 30.0 %collective-permute-start.21 = (bf16[4,240,512]{2,1,0:T(8,128)(2,1)}, bf16[4,240,512]{2,1,0:T(8,128)(2,1)S(1)}, u32[]{:S(2)}, u32[]{:S(2)}) collective-permute-start(bf16[4,240,512]{2,1,0:T(8,128)(2,1)} %get-tuple-element.98), channel_id=1, source_target_pairs={{0,1},{1,0},{2,3},{3,2},{4,5},{5,4},{6,7},{7,6},{8,9},{9,8},{10,11... | collective-permute-start | bytes 2949128 | tf_op jit(solution)/shard_map/ppermute | solution.py:808
  168.5 28.6 %collective-permute-start.20 = (bf16[240,1024]{1,0:T(8,128)(2,1)S(1)}, bf16[240,1024]{1,0:T(8,128)(2,1)S(1)}, u32[]{:S(2)}, u32[]{:S(2)}) collective-permute-start(bf16[240,1024]{1,0:T(8,128)(2,1)S(1)} %add_convert_fusion), channel_id=1, source_target_pairs={{0,6},{2,4},{4,2},{6,0},{1,7},{3,5},{5,3},{7,1},{8,14},{10,12},{12... | collective-permute-start | bytes 1474568 | tf_op jit(solution)/shard_map/ppermute | solution.py:808
  171.2 25.9 %collective-permute-start.18 = (bf16[240,1024]{1,0:T(8,128)(2,1)S(1)}, bf16[240,1024]{1,0:T(8,128)(2,1)S(1)}, u32[]{:S(2)}, u32[]{:S(2)}) collective-permute-start(bf16[240,1024]{1,0:T(8,128)(2,1)S(1)} %add_convert_fusion.2), channel_id=1, source_target_pairs={{0,2},{2,0},{1,3},{3,1},{4,6},{6,4},{5,7},{7,5},{8,10},{10,8},{9,1... | collective-permute-start | bytes 1474568 | tf_op jit(solution)/shard_map/ppermute | solution.py:808
  172.6 24.5 %collective-permute-start.19 = (bf16[240,1024]{1,0:T(8,128)(2,1)}, bf16[240,1024]{1,0:T(8,128)(2,1)}, u32[]{:S(2)}, u32[]{:S(2)}) collective-permute-start(bf16[240,1024]{1,0:T(8,128)(2,1)} %add_convert_fusion.1), channel_id=1, source_target_pairs={{0,4},{4,0},{1,5},{5,1},{2,6},{6,2},{3,7},{7,3},{8,12},{12,8},{9,1... | collective-permute-start | bytes 1474568 | tf_op jit(solution)/shard_map/ppermute | solution.py:808
  199.4 37.2 %collective-permute-start.26 = (bf16[240,1024]{1,0:T(8,128)(2,1)}, bf16[240,1024]{1,0:T(8,128)(2,1)S(1)}, u32[]{:S(2)}, u32[]{:S(2)}) collective-permute-start(bf16[240,1024]{1,0:T(8,128)(2,1)} %get-tuple-element.121), channel_id=1, source_target_pairs={{0,16},{8,24},{1,17},{9,25},{2,18},{10,26},{3,19},{11,27},{4,20},{... | collective-permute-start | bytes 1474568 | tf_op jit(solution)/shard_map/ppermute | solution.py:808
  206.1 27.8 %collective-permute-start.23 = (bf16[240,768]{1,0:T(8,128)(2,1)S(1)}, bf16[240,768]{1,0:T(8,128)(2,1)S(1)}, u32[]{:S(2)}, u32[]{:S(2)}) collective-permute-start(bf16[240,768]{1,0:T(8,128)(2,1)S(1)} %get-tuple-element.129), channel_id=1, source_target_pairs={{0,2},{2,0},{1,3},{3,1},{4,6},{6,4},{5,7},{7,5},{8,10},{10,8},{9,1... | collective-permute-start | bytes 1105928 | tf_op jit(solution)/shard_map/ppermute | solution.py:808
  207.7 26.2 %collective-permute-start.24 = (bf16[240,768]{1,0:T(8,128)(2,1)S(1)}, bf16[240,768]{1,0:T(8,128)(2,1)S(1)}, u32[]{:S(2)}, u32[]{:S(2)}) collective-permute-start(bf16[240,768]{1,0:T(8,128)(2,1)S(1)} %get-tuple-element.130), channel_id=1, source_target_pairs={{0,4},{4,0},{1,5},{5,1},{2,6},{6,2},{3,7},{7,3},{8,12},{12,8},{9,1... | collective-permute-start | bytes 1105928 | tf_op jit(solution)/shard_map/ppermute | solution.py:808
  209.2 24.7 %collective-permute-start.25 = (bf16[240,768]{1,0:T(8,128)(2,1)S(1)}, bf16[240,768]{1,0:T(8,128)(2,1)S(1)}, u32[]{:S(2)}, u32[]{:S(2)}) collective-permute-start(bf16[240,768]{1,0:T(8,128)(2,1)S(1)} %get-tuple-element.131), channel_id=1, source_target_pairs={{0,6},{2,4},{4,2},{6,0},{1,7},{3,5},{5,3},{7,1},{8,14},{10,12},{12... | collective-permute-start | bytes 1105928 | tf_op jit(solution)/shard_map/ppermute | solution.py:808
  235.1 36.7 %collective-permute-start.31 = (bf16[240,768]{1,0:T(8,128)(2,1)S(1)}, bf16[240,768]{1,0:T(8,128)(2,1)S(1)}, u32[]{:S(2)}, u32[]{:S(2)}) collective-permute-start(bf16[240,768]{1,0:T(8,128)(2,1)S(1)} %get-tuple-element.119), channel_id=1, source_target_pairs={{16,0},{24,8},{17,1},{25,9},{18,2},{26,10},{19,3},{27,11},{20,4},{... | collective-permute-start | bytes 1105928 | tf_op jit(solution)/shard_map/ppermute | solution.py:808
  239.1 15.0 %collective-permute-start.28 = (bf16[240,256]{1,0:T(8,128)(2,1)S(1)}, bf16[240,256]{1,0:T(8,128)(2,1)S(1)}, u32[]{:S(2)}, u32[]{:S(2)}) collective-permute-start(bf16[240,256]{1,0:T(8,128)(2,1)S(1)} %get-tuple-element.123), channel_id=1, source_target_pairs={{0,2},{2,0},{1,3},{3,1},{4,6},{6,4},{5,7},{7,5},{8,10},{10,8},{9,1... | collective-permute-start | bytes 368648 | tf_op jit(solution)/shard_map/ppermute | solution.py:808
  240.7 13.4 %collective-permute-start.29 = (bf16[240,256]{1,0:T(8,128)(2,1)S(1)}, bf16[240,256]{1,0:T(8,128)(2,1)S(1)}, u32[]{:S(2)}, u32[]{:S(2)}) collective-permute-start(bf16[240,256]{1,0:T(8,128)(2,1)S(1)} %get-tuple-element.124), channel_id=1, source_target_pairs={{0,4},{4,0},{1,5},{5,1},{2,6},{6,2},{3,7},{7,3},{8,12},{12,8},{9,1... | collective-permute-start | bytes 368648 | tf_op jit(solution)/shard_map/ppermute | solution.py:808
  242.2 11.9 %collective-permute-start.30 = (bf16[240,256]{1,0:T(8,128)(2,1)S(1)}, bf16[240,256]{1,0:T(8,128)(2,1)S(1)}, u32[]{:S(2)}, u32[]{:S(2)}) collective-permute-start(bf16[240,256]{1,0:T(8,128)(2,1)S(1)} %get-tuple-element.125), channel_id=1, source_target_pairs={{0,6},{2,4},{4,2},{6,0},{1,7},{3,5},{5,3},{7,1},{8,14},{10,12},{12... | collective-permute-start | bytes 368648 | tf_op jit(solution)/shard_map/ppermute | solution.py:808
  263.7 12.8 %collective-permute-start.39 = (bf16[256,256]{1,0:T(8,128)(2,1)S(1)}, bf16[256,256]{1,0:T(8,128)(2,1)S(1)}, u32[]{:S(2)}, u32[]{:S(2)}) collective-permute-start(bf16[256,256]{1,0:T(8,128)(2,1)S(1)} %fusion.18), channel_id=1, source_target_pairs={{8,0},{16,24},{9,1},{17,25},{10,2},{18,26},{11,3},{19,27},{12,4},{... | collective-permute-start | bytes 393224 | tf_op jit(solution)/shard_map/ppermute | solution.py:808
  (30 other events, 192.3 us)
where the time goes:
time: 286 us; the launch traced here: 283 us
  Pallas kernels  157 us (55%)
  starting transfers between devices  59.7 us (21%)
  waiting for transfers between devices  38.6 us (13%)
  other arithmetic  16.6 us (6%)
  local copies, waits for them, and re-layouts  9.09 us (3%)
    pallas_call x8, Pallas kernels, call_kernel(): pl.pallas_call(run, name=name, grid_spec=pltpu.PrefetchScalarGridSpec(num...  157 us
    ppermute x40, starting transfers between devices, move(): return lambda value: lax.ppermute(value, axis, perm)  59.7 us
    ppermute x40, waiting for transfers between devices, move(): return lambda value: lax.ppermute(value, axis, perm)  38.6 us
  transfers between devices with their start and end apart: 40, of which 12 were waited for; matrix products, arithmetic and copies ran while one was open for 7% of the time, Pallas kernels for 33%

commit v1 on v0

--- a/solution.py
+++ b/solution.py
@@ -90,7 +90,7 @@
 PLANE_END = [STARTS[(plane + 1) * IN_PLANE - 1] + BLOCK for plane in range(PLANES)]
 VEC_AT = ROW_VEC - STARTS[-1]
 
-VMEM = pltpu.CompilerParams(vmem_limit_bytes=60 * MB)
+VMEM = pltpu.CompilerParams(vmem_limit_bytes=62 * MB)
 
 
 def whole(shape, single=True):
@@ -106,18 +106,15 @@
 
 
 class Piece:
-    def __init__(self, array, blocks, other, column):
-        self.array, self.blocks, self.other, self.column = array, blocks, other, column
-
-
-def place_piece(target, base, where, piece, source, lowest):
-    width = min(source.shape[-1], target.shape[-1] - piece.column)
-
+    def __init__(self, array, blocks, other):
+        self.array, self.blocks, self.other = array, blocks, other
+
+
+def place_piece(target, base, where, piece, block_of, lowest):
     def place(index, plane, spot):
         at = share_row(where, plane, spot, piece.other) - base
         rows = pl.ds(pl.multiple_of(at, TILE_ROWS), BLOCK)
-        cols = slice(piece.column, piece.column + width)
-        target[rows, cols] = target[rows, cols] + source[index, :BLOCK, :width]
+        target[rows, :] = target[rows, :] + block_of(index)
 
     for index, (plane, spot) in enumerate(piece.blocks):
         if not isinstance(plane, tuple):
@@ -158,12 +155,27 @@
     return results[:outputs], results[outputs:]
 
 
-def emit_blocks(source, base, plane, where, keep, send):
-    @pl.loop(0, HALF)
-    def _(spot):
+def emit_copies(source, base, plane, where, keep, send, sems):
+    copies = []
+    for spot in range(HALF):
         for out, other in ((keep, False), (send, True)):
-            at = share_row(where, plane, spot, other) - base
-            out[spot] = source[pl.ds(pl.multiple_of(at, TILE_ROWS), BLOCK), :]
+            at = pl.multiple_of(share_row(where, plane, spot, other) - base, TILE_ROWS)
+            copy = pltpu.make_async_copy(source.at[pl.ds(at, BLOCK), :], out.at[spot], sems.at[len(copies)])
+            copies.append(copy)
+    return copies
+
+
+def start_all(copies):
+    for copy in copies:
+        copy.start()
+
+
+def wait_all(copies):
+    for copy in copies:
+        copy.wait()
+
+
+COPY_SEMS = pltpu.SemaphoreType.DMA((IN_PLANE,))
 
 
 def split_three(values):
@@ -256,6 +268,10 @@
             extra[rows, cols] = jnp.concatenate(lines, 0).T.astype(BF16)
 
 
+def block_columns(source, index):
+    return source[index, :BLOCK, :GROUP]
+
+
 def forward_body(first, pieces, longs, where, rows_in, *rest):
     sources, rest = rest[: len(pieces)], rest[len(pieces) :]
     if first:
@@ -268,7 +284,7 @@
     def _():
         weights[...] = jnp.zeros_like(weights)
         for piece, source in zip(pieces, sources):
-            place_piece(weights, 0, where, piece, source, True)
+            place_piece(weights, 0, where, piece, functools.partial(block_columns, source), True)
         w_three[...] = weights[:ROW_OUT, :]
         w_out[...] = weights[ROW_OUT:, :]
         if first:
@@ -406,7 +422,7 @@
 
 
 def backward_body(steps, where, query, key, value, extra, attended, grad, hidden, late, *refs):
-    grad_query, grad_key, grad_value, keep, send, total, rows = refs
+    grad_query, grad_key, grad_value, keep, send, total, rows, sems = refs
     step = pl.program_id(0)
     attend_back_rows(query, key, value, extra, attended, grad, grad_query, grad_key, grad_value)
     three = jnp.concatenate([grad_query[...], grad_key[...], grad_value[...]], 1)
@@ -425,7 +441,9 @@
         for part, at in enumerate((ROW_QUERY, ROW_KEY, ROW_VALUE)):
             rows[at : at + D, :] = total[:, part * GROUP : (part + 1) * GROUP].astype(BF16)
         rows[ROW_OUT:, :] = late[...]
-        emit_blocks(rows, 0, 0, where, keep, send)
+        copies = emit_copies(rows, 0, 0, where, keep, send, sems)
+        start_all(copies)
+        wait_all(copies)
 
 
 def backward_group(group, where, query, key, value, extra, attended, grad, hidden, late, through):
@@ -443,7 +461,7 @@
             pl.BlockSpec((LONG, D), lambda s, *refs: (s, 0)),
             pl.BlockSpec((late.shape[0], GROUP), lambda s, *refs: (0, group), pipeline_mode=pl.Buffered(1)),
         ],
-        [part] * 3 + [whole(block)] * 2,
+        [part] * 3 + [UNREAD] * 2,
         [jax.ShapeDtypeStruct((total, GROUP), BF16)] * 3 + [jax.ShapeDtypeStruct(block, BF16)] * 2,
         (steps,),
         "backward_group",
@@ -451,12 +469,15 @@
         scratch=[
             pltpu.VMEM((D, 3 * GROUP), F32),
             pltpu.VMEM((ROW_OUT + late.shape[0], GROUP), BF16),
+            COPY_SEMS,
         ],
     )
 
 
 MID_ROWS = 512
 HALF_ROWS = 256
+STAGE_ROWS = 256
+STAGE = 8
 CHUNKS = FF // D
 TANH_SCALE = math.sqrt(2.0 / math.pi)
 
@@ -480,18 +501,31 @@
 def middle_body(steps, pieces, where, tok, grad_out, hidden_a, *refs):
     att_refs, wo_refs, refs = refs[:GROUPS], refs[GROUPS : 2 * GROUPS], refs[2 * GROUPS :]
     sources, refs = refs[: len(pieces)], refs[len(pieces) :]
-    (outputs, grad_middle_ref, grad_za_ref, grad_attended, hid_f_ref, chunks_ref, grad_f_ref) = refs[:7]
-    (grad_zf_ref, grad_a_ref, d_vec, gate_copy, weights, wide, slope, s_vec) = refs[7:]
+    (outputs, grad_middle_ref, grad_za_ref, grad_attended, hid_f_ref, grad_zf_ref, grad_a_ref, gate_copy) = refs[:8]
+    (keep_three, send_three, keep_two, send_two, carry, weights, wide, slope, s_vec, kept, s_hid_f, s_grad_f) = refs[8:-3]
+    load_sems, sems_three, sems_two = refs[-3:]
     step = pl.program_id(0)
     base = ROW_OUT
 
     @pl.when(step == 0)
     def _():
+        staged = []
+        for piece, source in zip(pieces, sources):
+            for index in range(len(piece.blocks)):
+                slot = len(staged)
+                to = kept.at[slot // STAGE, pl.ds(slot % STAGE * STAGE_ROWS, BLOCK), :]
+                staged.append((to, pltpu.make_async_copy(source.at[index, pl.ds(0, BLOCK), :], to, load_sems.at[slot])))
+                staged[-1][1].start()
         weights[...] = jnp.zeros_like(weights)
         for group in range(GROUPS):
             weights[: PLANE_END[0] - ROW_OUT, group * GROUP : (group + 1) * GROUP] = wo_refs[group][...]
-        for piece, source in zip(pieces, sources):
-            place_piece(weights, base, where, piece, source, False)
+        at_slot = 0
+        for piece in pieces:
+            count = len(piece.blocks)
+            here = staged[at_slot : at_slot + count]
+            wait_all([copy for unused, copy in here])
+            place_piece(weights, base, where, piece, lambda index, here=here: here[index][0][...], False)
+            at_slot += count
         shuffle = spread_matrix(256)
         for block in range(FF // 256):
             at = ROW_IN - base + block * 256
@@ -508,7 +542,11 @@
     vecs = weights[ROW_VEC - base : ROW_VEC - base + VEC_ROWS, :].astype(F32)
     chunks = [slice(chunk * D, (chunk + 1) * D) for chunk in range(CHUNKS)]
 
-    def part(here):
+    first_row = pl.multiple_of(step * MID_ROWS, MID_ROWS)
+
+    def part(at):
+        here = slice(at, at + HALF_ROWS)
+        there = pl.ds(first_row + at, HALF_ROWS)
         hid_a = hidden_a[here, :]
         att = jnp.concatenate([ref[here, :] for ref in att_refs], 1)
         grad = grad_out[here, :].astype(F32)
@@ -521,6 +559,7 @@
         normed, inv_std = layer_stats(middle)
         hid_f = (normed * vecs[4:5] + vecs[5:6]).astype(BF16)
         hid_f_ref[here, :] = hid_f
+        s_hid_f[there, :] = hid_f
         yield
         gate_f = dot_nn(hid_f, gate_ffn[...])
         pre = dot_nn(hid_f, wide[0])
@@ -535,7 +574,7 @@
             slope[here, cols] = half + (0.5 * pre) * (1.0 - bend * bend) * (
                 TANH_SCALE + (3.0 * 0.044715 * TANH_SCALE) * square
             )
-            chunks_ref[chunk, here, :] = active
+            kept[chunk, there, :] = active
             yield
             if chunk + 1 < CHUNKS:
                 pre = dot_nn(hid_f, wide[chunk + 1])
@@ -545,7 +584,7 @@
         outputs[here, :] = (middle + gate_f * branch_f).astype(BF16)
         grad_branch_f = (grad * gate_f).astype(BF16)
         grad_zf = (grad * branch_f * gate_f * (1.0 - gate_f)).astype(BF16)
-        grad_f_ref[here, :] = grad_branch_f
+        s_grad_f[there, :] = grad_branch_f
         grad_zf_ref[here, :] = grad_zf
         s_vec[6] += fold_rows(grad_branch_f.astype(F32))
         s_vec[7] += fold_rows(grad_zf.astype(F32))
@@ -555,7 +594,7 @@
         yield
         for chunk, cols in enumerate(chunks):
             grad_pre = (grad_active * slope[here, cols]).astype(BF16)
-            chunks_ref[CHUNKS + chunk, here, :] = grad_pre
+            kept[CHUNKS + chunk, there, :] = grad_pre
             s_vec[8 + chunk] += fold_rows(grad_pre.astype(F32))
             yield
             if chunk + 1 < CHUNKS:
@@ -576,18 +615,36 @@
         grad_attended[here, :] = dot_nt(grad_branch_a, w_out[...]).astype(BF16)
         yield
 
-    interleave([part(slice(at, at + HALF_ROWS)) for at in range(0, MID_ROWS, HALF_ROWS)])
+    interleave([part(at) for at in range(0, MID_ROWS, HALF_ROWS)])
 
     @pl.when(step == steps - 1)
     def _():
-        d_vec[...] = jnp.sum(s_vec[...], 1).astype(BF16)
+        for chunk in range(CHUNKS):
+            at = ROW_DOWN - base + chunk * D
+            weights[at : at + D, :] = dot_tn(kept[chunk], s_grad_f[...]).astype(BF16)
+        weights[ROW_VEC - base :, :] = jnp.sum(s_vec[...], 1).astype(BF16)
+        copies = emit_copies(weights, base, 3, where, keep_three, send_three, sems_three)
+        start_all(copies)
+        for chunk in range(CHUNKS):
+            wide[chunk] = dot_tn(s_hid_f[...], kept[CHUNKS + chunk]).astype(BF16)
+        shuffle = spread_matrix(256)
+        for block in range(FF // 256):
+            parts = [wide[chunk, block * 64 : (block + 1) * 64, :] for chunk in range(CHUNKS)]
+            at = ROW_IN - base + block * 256
+            weights[at : at + 256, :] = dot_tn(shuffle, jnp.concatenate(parts, 0)).astype(BF16)
+        last = emit_copies(weights, base, 2, where, keep_two, send_two, sems_two)
+        start_all(last)
+        carry[...] = weights[ROW_IN - base : PLANE_END[1] - base, :]
+        wait_all(copies)
+        wait_all(last)
 
 
 def middle_part(where, tokens, grad_out, hidden_a, attended, w_outs, pieces):
     total = tokens.shape[0]
     steps = total // MID_ROWS
+    carry = PLANE_END[1] - ROW_IN
     rows_at = lambda width: pl.BlockSpec((MID_ROWS, width), lambda i, *refs: (i, 0))
-    shape = lambda width, kind=BF16: jax.ShapeDtypeStruct((total, width), kind)
+    shape = lambda kind=BF16: jax.ShapeDtypeStruct((total, D), kind)
     results, unused = call_kernel(
         functools.partial(middle_body, steps, pieces),
         [where, tokens, grad_out, hidden_a, *attended, *w_outs, *[piece.array for piece in pieces]],
@@ -595,100 +652,48 @@
         [rows_at(D)] * 3
         + [rows_at(GROUP)] * GROUPS
         + [whole(w_outs[0].shape)] * GROUPS
-        + [whole(piece.array.shape) for piece in pieces],
-        [rows_at(D)] * 5
-        + [pl.BlockSpec((2 * CHUNKS, MID_ROWS, D), lambda i, *refs: (0, i, 0))]
-        + [rows_at(D)] * 3
-        + [whole((VEC_ROWS, D)), whole((D, D))],
-        [shape(D), shape(D, F32), shape(D), shape(D), shape(D)]
-        + [jax.ShapeDtypeStruct((2 * CHUNKS, total, D), BF16)]
-        + [shape(D)] * 3
-        + [jax.ShapeDtypeStruct((VEC_ROWS, D), BF16), jax.ShapeDtypeStruct((D, D), BF16)],
+        + [UNREAD] * len(pieces),
+        [rows_at(D)] * 7 + [whole((D, D))] + PLANE_SPEC * 2 + [whole((carry, D))],
+        [shape(), shape(F32)]
+        + [shape()] * 5
+        + [jax.ShapeDtypeStruct((D, D), BF16)]
+        + PLANE_OUT * 2
+        + [jax.ShapeDtypeStruct((carry, D), BF16)],
         (steps,),
         "middle_part",
-        (24e9, 50e6, 4e6),
+        (33e9, 50e6, 4e6),
         scratch=[
             pltpu.VMEM((ALL_ROWS - ROW_OUT, D), BF16),
             pltpu.VMEM((CHUNKS, D, D), BF16),
             pltpu.VMEM((MID_ROWS, FF), F32),
             pltpu.VMEM((VEC_ROWS, 8, D), F32),
+            pltpu.VMEM((2 * CHUNKS, total, D), BF16),
+            pltpu.VMEM((total, D), BF16),
+            pltpu.VMEM((total, D), BF16),
+            pltpu.SemaphoreType.DMA((SHARES,)),
+            COPY_SEMS,
+            COPY_SEMS,
         ],
     )
     return results
 
 
 PLANE_OUT = [jax.ShapeDtypeStruct((HALF, BLOCK, D), BF16)] * 2
-PLANE_SPEC = [whole((HALF, BLOCK, D))] * 2
-
-
-def ffn_body(where, chunk, grad_f, hidden_f, d_vec, keep_three, send_three, keep_two, send_two, carry, rows, wide):
-    step = pl.program_id(0)
-
-    @pl.when(step < CHUNKS)
-    def _():
-        at = pl.multiple_of(ROW_DOWN - ROW_IN + step * D, D)
-        rows[pl.ds(at, D), :] = dot_tn(chunk[...], grad_f[...]).astype(BF16)
-
-    @pl.when(step >= CHUNKS)
-    def _():
-        wide[step - CHUNKS] = dot_tn(hidden_f[...], chunk[...]).astype(BF16)
-
-    @pl.when(step == CHUNKS - 1)
-    def _():
-        rows[ROW_VEC - ROW_IN :, :] = d_vec[...]
-        emit_blocks(rows, ROW_IN, 3, where, keep_three, send_three)
-
-    @pl.when(step == 2 * CHUNKS - 1)
-    def _():
-        shuffle = spread_matrix(256)
-
-        @pl.loop(0, FF // 256)
-        def _(block):
-            quarter = pl.ds(pl.multiple_of(block * 64, 64), 64)
-            parts = [wide[chunk, quarter, :] for chunk in range(CHUNKS)]
-            to = pl.ds(pl.multiple_of(block * 256, 256), 256)
-            rows[to, :] = dot_tn(shuffle, jnp.concatenate(parts, 0)).astype(BF16)
-
-        emit_blocks(rows, ROW_IN, 2, where, keep_two, send_two)
-        carry[...] = rows[: PLANE_END[1] - ROW_IN, :]
-
-
-def ffn_gradient(where, chunks, grad_f, hidden_f, d_vec):
-    total = chunks.shape[1]
-    carry = PLANE_END[1] - ROW_IN
-    results, unused = call_kernel(
-        ffn_body,
-        [where, chunks, grad_f, hidden_f, d_vec],
-        [],
-        [
-            pl.BlockSpec((pl.Squeezed(), total, D), lambda i, *refs: (i, 0, 0)),
-            whole((total, D)),
-            whole((total, D)),
-            whole((VEC_ROWS, D)),
-        ],
-        PLANE_SPEC * 2 + [whole((carry, D))],
-        PLANE_OUT * 2 + [jax.ShapeDtypeStruct((carry, D), BF16)],
-        (2 * CHUNKS,),
-        "ffn_gradient",
-        (8.6e9, 24e6, 0),
-        scratch=[
-            pltpu.VMEM((ALL_ROWS - ROW_IN, D), BF16),
-            pltpu.VMEM((CHUNKS, D, D), BF16),
-        ],
-    )
-    return results
+PLANE_SPEC = [UNREAD] * 2
 
 
 def gates_body(where, *refs):
     att_refs, refs = refs[:GROUPS], refs[GROUPS:]
-    hidden_a, hidden_f, grad_a, grad_za, grad_zf, late, keep, send, carry, rows = refs
+    hidden_a, hidden_f, grad_a, grad_za, grad_zf, late, keep, send, carry, rows, sems = refs
     att = jnp.concatenate([ref[...] for ref in att_refs], 1)
     rows[:D, :] = dot_tn(att, grad_a[...]).astype(BF16)
     rows[D : 2 * D, :] = dot_tn(hidden_a[...], grad_za[...]).astype(BF16)
     rows[2 * D : 3 * D, :] = dot_tn(hidden_f[...], grad_zf[...]).astype(BF16)
     rows[3 * D :, :] = late[...]
-    emit_blocks(rows, ROW_OUT, 1, where, keep, send)
+    copies = emit_copies(rows, ROW_OUT, 1, where, keep, send, sems)
+    start_all(copies)
     carry[...] = rows[: PLANE_END[0] - ROW_OUT, :]
+    wait_all(copies)
 
 
 def gates_gradient(where, attended, hidden_a, hidden_f, grad_a, grad_za, grad_zf, late, through):
@@ -704,7 +709,7 @@
         (1,),
         "gates_gradient",
         (3.2e9, 14e6, 0),
-        scratch=[pltpu.VMEM((3 * D + late.shape[0], D), BF16)],
+        scratch=[pltpu.VMEM((3 * D + late.shape[0], D), BF16), COPY_SEMS],
     )
 
 
@@ -770,10 +775,9 @@
     later("forward1", passed)
     groups = [kept, second]
     attended = [group[3] for group in groups]
-    (outputs, grad_middle, grad_za, grad_attended, hidden_f, chunks, grad_f, grad_zf, grad_a, d_vec, gate_attn) = (
+    (outputs, grad_middle, grad_za, grad_attended, hidden_f, grad_zf, grad_a, gate_attn, keep, send, *plane, carry) = (
         middle_part(where, rows, grads_in, hidden_a, attended, [group[6] for group in groups], middle_pieces())
     )
-    keep, send, *plane, carry = ffn_gradient(where, chunks, grad_f, hidden_f, d_vec)
     collect(3, keep, send)
     collect(2, *plane)
     (*plane, carry), passed = gates_gradient(
@@ -821,37 +825,38 @@
     swap_xy = move(("x", "y"), 4, lambda i: 3 - i)
     z_one = move("z", 4, lambda i: i ^ 1)
     z_two = move("z", 4, lambda i: i ^ 2)
-    z_ends = move("z", 4, lambda i: {0: 2, 3: 1}.get(i))
-    z_mid = move("z", 4, lambda i: {1: 2, 2: 1}.get(i))
-    z_out = move("z", 4, lambda i: {1: 0, 2: 3}.get(i))
-
     inside = z < 4
     vec = block[VEC_AT : VEC_AT + VEC_ROWS]
     mine = jnp.concatenate([block, jnp.where(me == SHARES - 1, vec, jnp.zeros_like(vec))], 0)
-    held = jnp.where(ends, mine, z_ends(mine))
-    out_first, got_mid = z_out(block), z_mid(block)
-    got = z_one(jnp.concatenate([held, jnp.where(inside, got_mid, out_first)], 0))
-    other, out_second = got[: BLOCK + VEC_ROWS], got[BLOCK + VEC_ROWS :]
-    vec = jnp.where(odd, held, other)[BLOCK:]
-    first = jnp.concatenate([jnp.where(z == 2, held, other)[:BLOCK], vec], 0)[None]
-    one = jnp.where(z == 0, out_first, jnp.where(z == 1, held[:BLOCK], jnp.where(z == 2, got_mid, out_second)))
-    two = jnp.where(z == 0, out_second, jnp.where(z == 1, got_mid, jnp.where(z == 2, other[:BLOCK], out_first)))
-    both = jnp.stack([one, two])
+    step_one = move("z", 4, {0: 2, 1: 0, 2: 3, 3: 1}.get)(mine)
+    held = jnp.where(ends, mine, step_one)
+    step_two = z_one(held)
+    step_three = z_two(jnp.where(ends, step_one[:BLOCK], block))
+    vec = jnp.where(odd, held, step_two)[BLOCK:]
+    first = jnp.where(inside, jnp.where(z == 2, step_one, step_two)[:BLOCK], step_three)
+    first = jnp.concatenate([first, vec], 0)[None]
+    both = jnp.stack([jnp.where(z == 2, step_two, step_one)[:BLOCK], step_three])
 
     def in_plane(parts, planes):
         near = jnp.concatenate(parts, 0)
         blocks = [(plane, spot) for spot in range(HALF) for plane in planes]
-        return [Piece(near, blocks, False, 0), Piece(swap_c(near), blocks, True, 0)]
+        return [Piece(near, blocks, False), Piece(swap_c(near), blocks, True)]
 
     own = block[None]
     pieces = in_plane([own, swap_y(own), swap_x(own), swap_xy(own)], ((0,),))
     pieces += in_plane([first, swap_y(first), swap_x(first), swap_xy(first)], ((4,),))
     around = {"both": [swap_y(both), swap_x(both), swap_xy(both)]}
     top = {"both": both[:, :TILE_ROWS]}
+    pair = ((5,), (6,))
+    blocks = [(plane, 0) for plane in pair]
+    both_pieces = [Piece(both, blocks, False), Piece(swap_c(both), blocks, True)]
 
     def middle_pieces():
-        mine = jnp.concatenate([top["both"], both[:, TILE_ROWS:]], 1)
-        return pieces + in_plane([mine] + around["both"], ((5,), (6,)))
+        late = jnp.pad(top["both"], ((0, 0), (0, BLOCK - TILE_ROWS), (0, 0)))
+        parts = around["both"]
+        near = jnp.concatenate([jnp.where(inside, parts[0], late), *parts[1:]], 0)
+        blocks = [(plane, spot) for spot in range(1, HALF) for plane in pair]
+        return pieces + both_pieces + [Piece(near, blocks, False), Piece(swap_c(near), blocks, True)]
 
     early, late = ("first", 0), ("first", 1)
     arrived, at_chip, held = {}, {}, {}
@@ -917,7 +922,7 @@
         if name == "last":
             held["give"], held["mine"], held["lower"], at_chip["late"] = passed
 
-    planes = [jnp.where(z == 0, 3, 0), jnp.where(z == 1, 3, 1), jnp.where(z == 2, 3, 2)]
+    planes = [jnp.where(z == 0, 3, 0), jnp.where(z == 0, 1, jnp.where(z == 3, 2, 3)), jnp.where(z < 2, 2, 1)]
     where = jnp.stack([z, x, y, c, *planes]).astype(jnp.int32)
     outputs, input_grad, d_vec = local_part(
         where,
@@ -940,7 +945,7 @@
     gains = gains + swap_c(gains)
     gains = (gains + swap_x(gains) + swap_y(gains) + swap_xy(gains)).reshape(2 * GROUPS, GROUP)
     lines = jnp.pad(gains.astype(BF16), ((0, TILE_ROWS - 2 * GROUPS), (0, 0)))
-    message = jnp.concatenate([low.astype(BF16), lines], 0)
+    message = jnp.concatenate([jnp.where(inside, low, given[:, :GROUP]).astype(BF16), lines], 0)
     for step in ({3: 0, 0: 3}, {2: 0, 1: 3}, {1: 0, 2: 3}):
         got = move("z", 4, step.get)(message).astype(F32)
         low = low + got[:BLOCK]
@@ -970,15 +975,15 @@
             piece = merged[STARTS[index] : end]
             blocks.append(jnp.pad(piece, ((0, BLOCK - piece.shape[0]), (0, 0))))
         spots = [(plane, spot) for spot in range(HALF)]
-        near.append(Piece(jnp.stack(blocks[0::2]), spots, False, 0))
-        far.append(Piece(jnp.stack(blocks[1::2]), spots, True, 0))
+        near.append(Piece(jnp.stack(blocks[0::2]), spots, False))
+        far.append(Piece(jnp.stack(blocks[1::2]), spots, True))
     vec = merged[ROW_VEC : ROW_VEC + VEC_ROWS]
     first_pieces = []
     for piece in (near[0], far[0]):
         lines = jnp.zeros((HALF, VEC_ROWS, D), BF16)
         if piece is near[0]:
             lines = lines.at[0].set(vec)
-        first_pieces.append(Piece(jnp.concatenate([piece.array, lines], 1), piece.blocks, piece.other, 0))
+        first_pieces.append(Piece(jnp.concatenate([piece.array, lines], 1), piece.blocks, piece.other))
     by_share = [None] * SHARES
 
     halves = []

time: 286 us -> 272 us (0.951)
  Pallas kernels: 157 us -> 149 us
  starting transfers between devices: 59.7 us -> 52.3 us
  waiting for transfers between devices: 38.6 us -> 34.4 us
  local copies, waits for them, and re-layouts: 9.09 us -> 12.7 us
    pallas_call x8 -> x7, Pallas kernels: 157 us -> 149 us  [call_kernel(): pl.pallas_call(run, name=name, grid_spec=pltpu.PrefetchScalarGridSpec(num...]
    ppermute x40, starting transfers between devices: 59.7 us -> 52.3 us  [move(): return lambda value: lax.ppermute(value, axis, perm)]
    ppermute x40, waiting for transfers between devices: 38.6 us -> 34.4 us  [move(): return lambda value: lax.ppermute(value, axis, perm)]
  transfers between devices with their start and end apart: 40 -> 40, of which waited for: 12 -> 14; matrix products, arithmetic and copies ran while one was open for 7% -> 8% of each run, Pallas kernels for 33% -> 35%
where the time goes in v1:
time: 272 us; the launch traced here: 269 us
  Pallas kernels  149 us (55%)
  starting transfers between devices  52.3 us (19%)
  waiting for transfers between devices  34.4 us (13%)
  other arithmetic  18.5 us (7%)
  local copies, waits for them, and re-layouts  12.7 us (5%)
    pallas_call x7, Pallas kernels, call_kernel(): pl.pallas_call(run, name=name, grid_spec=pltpu.PrefetchScalarGridSpec(num...  149 us
    ppermute x40, starting transfers between devices, move(): return lambda value: lax.ppermute(value, axis, perm)  52.3 us
    ppermute x40, waiting for transfers between devices, move(): return lambda value: lax.ppermute(value, axis, perm)  34.4 us
    convert_element_type x7, other arithmetic, send_around(): part.append((keep + got).astype(BF16))  5.84 us
  transfers between devices with their start and end apart: 40, of which 14 were waited for; matrix products, arithmetic and copies ran while one was open for 8% of the time, Pallas kernels for 35%

profile of v1, /device:TPU:0, one launch (start us, length us, event | category | flops | bytes accessed | tf_op | source)
XLA Modules:
  0.0 268.8 jit_solution(11137535424370055791)
XLA Ops:
  2.2 4.1 %collective-permute-start.4 = (bf16[256,512]{1,0:T(8,128)(2,1)S(1)}, bf16[256,512]{1,0:T(8,128)(2,1)S(1)}, u32[]{:S(2)}, u32[]{:S(2)}) collective-permute-start(bf16[256,512]{1,0:T(8,128)(2,1)S(1)} %constant_dynamic-update-slice_fusion.4), channel_id=1, source_target_pairs={{0,16},{8,0},{16,24},{24,8},{1,17},{9,1},{17,25},{25,9},{2,18},{10... | collective-permute-start | bytes 786440 | tf_op jit(solution)/shard_map/ppermute | solution.py:812
  6.3 5.6 %collective-permute-done.4 = bf16[256,512]{1,0:T(8,128)(2,1)S(1)} collective-permute-done((bf16[256,512]{1,0:T(8,128)(2,1)S(1)}, bf16[256,512]{1,0:T(8,128)(2,1)S(1)}, u32[]{:S(2)}, u32[]{:S(2)}) %collective-permute-start.4) | collective-permute-done | bytes 262176 | tf_op jit(solution)/shard_map/ppermute | solution.py:812
  11.8 2.4 collective-permute-start.5
  19.3 5.0 %collective-permute-done.6 = bf16[240,512]{1,0:T(8,128)(2,1)S(1)} collective-permute-done((bf16[240,512]{1,0:T(8,128)(2,1)S(1)}, bf16[240,512]{1,0:T(8,128)(2,1)S(1)}, u32[]{:S(2)}, u32[]{:S(2)}) %collective-permute-start.6) | collective-permute-done | bytes 245792 | tf_op jit(solution)/shard_map/ppermute | solution.py:812
  25.1 2.5 collective-permute-start.9
  28.7 2.5 collective-permute-start.2
  31.2 4.2 %collective-permute-done.9 = bf16[1,256,512]{2,1,0:T(8,128)(2,1)S(1)} collective-permute-done((bf16[1,256,512]{2,1,0:T(8,128)(2,1)S(1)}, bf16[1,256,512]{2,1,0:T(8,128)(2,1)S(1)}, u32[]{:S(2)}, u32[]{:S(2)}) %collective-permute-start.9) | collective-permute-done | bytes 262176 | tf_op jit(solution)/shard_map/ppermute | solution.py:812
  35.4 4.9 %collective-permute-done.8 = bf16[1,256,512]{2,1,0:T(8,128)(2,1)S(1)} collective-permute-done((bf16[1,256,512]{2,1,0:T(8,128)(2,1)S(1)}, bf16[1,256,512]{2,1,0:T(8,128)(2,1)S(1)}, u32[]{:S(2)}, u32[]{:S(2)}) %collective-permute-start.8) | collective-permute-done | bytes 262176 | tf_op jit(solution)/shard_map/ppermute | solution.py:812
  40.5 2.3 collective-permute-done.2
  44.5 2.5 collective-permute-start.14
  49.6 14.4 %forward_group.2 = (bf16[2048,256]{1,0:T(8,128)(2,1)}, bf16[2048,256]{1,0:T(8,128)(2,1)}, bf16[2048,256]{1,0:T(8,128)(2,1)}, bf16[2048,256]{1,0:T(8,128)(2,1)}, ...) custom-call(s32[2]{0:T(128)} %bitcast.122, ...), custom_call_target="tpu_custom_call" | custom-call | flops 8000000000 | bytes 12000000 | tf_op jit(solution)/shard_map/forward_group/pallas_call | solution.py:140
  64.0 12.8 %forward_group.3 = (bf16[2048,256]{1,0:T(8,128)(2,1)}, bf16[2048,256]{1,0:T(8,128)(2,1)}, bf16[2048,256]{1,0:T(8,128)(2,1)}, bf16[2048,256]{1,0:T(8,128)(2,1)}, ...) custom-call(s32[2]{0:T(128)} %bitcast.123, ...), custom_call_target="tpu_custom_call", output_to_operand_aliasing={{7}: (7, {})} | custom-call | tf_op jit(solution)/shard_map/forward_group/pallas_call | solution.py:140
  79.9 3.3 %collective-permute-done.11.refs_13_ = bf16[2,240,512]{2,1,0:T(8,128)(2,1)S(1)} collective-permute-done((bf16[2,240,512]{2,1,0:T(8,128)(2,1)}, bf16[2,240,512]{2,1,0:T(8,128)(2,1)S(1)}, u32[]{:S(2)}, u32[]{:S(2)}) %collective-permute-start.11) | collective-permute-done | bytes 491552 | tf_op jit(solution)/shard_map/ppermute | solution.py:812
  84.5 54.1 %middle_part.1 = (bf16[2048,512]{1,0:T(8,128)(2,1)}, f32[2048,512]{1,0:T(8,128)}, bf16[2048,512]{1,0:T(8,128)(2,1)}, bf16[2048,512]{1,0:T(8,128)(2,1)}, bf16[204...) custom-call(s32[7]{0:T(128)} %stack.40.refs_1_.refs_0_, ...), custom_call_target="tpu_custom_call" | custom-call | flops 32999999488 | bytes 50000000 | tf_op jit(solution)/shard_map/middle_part/pallas_call | solution.py:140
  139.2 11.0 %gates_gradient.1 = (bf16[4,240,512]{2,1,0:T(8,128)(2,1)}, bf16[4,240,512]{2,1,0:T(8,128)(2,1)}, bf16[272,512]{1,0:T(8,128)(2,1)}, bf16[4,240,512]{2,1,0:T(8,128)(2,1)}, bf16[4,240,512]{2,1,0:T(8,128)(2,1)}) custom-call(s32[7]{0:T(128)} %stack.40.refs_1_.refs_0_, ...), custom_call_target="tpu_custom_call", output_to_operand_aliasing={{3}: (9, {}), {4}: (10, {})} | custom-call | flops 3200000000 | bytes 14000000 | tf_op jit(solution)/shard_map/gates_gradient/pallas_call | solution.py:140
  150.6 2.4 slice_bitcast_fusion.14
  154.9 2.6 collective-permute-start.20
  161.2 22.6 %backward_group.2 = (bf16[2048,256]{1,0:T(8,128)(2,1)}, bf16[2048,256]{1,0:T(8,128)(2,1)}, bf16[2048,256]{1,0:T(8,128)(2,1)}, bf16[4,240,256]{2,1,0:T(8,128)(2,1...) custom-call(s32[7]{0:T(128)} %stack.40.refs_1_.refs_0_, ...), custom_call_target="tpu_custom_call", output_to_operand_aliasing={{5}: (9, {})} | custom-call | flops 14000000000 | bytes 16000000 | tf_op jit(solution)/shard_map/backward_group/pallas_call | solution.py:140
  186.6 5.0 %collective-permute-start.26 = (bf16[240,1024]{1,0:T(8,128)(2,1)S(1)}, bf16[240,1024]{1,0:T(8,128)(2,1)S(1)}, u32[]{:S(2)}, u32[]{:S(2)}) collective-permute-start(bf16[240,1024]{1,0:T(8,128)(2,1)S(1)} %get-tuple-element.113), channel_id=1, source_target_pairs={{0,16},{8,24},{1,17},{9,25},{2,18},{10,26},{3,19},{11,27},{4,20},{... | collective-permute-start | bytes 1474568 | tf_op jit(solution)/shard_map/ppermute | solution.py:812
  197.4 22.7 %backward_group.3 = (bf16[2048,256]{1,0:T(8,128)(2,1)}, bf16[2048,256]{1,0:T(8,128)(2,1)}, bf16[2048,256]{1,0:T(8,128)(2,1)}, bf16[4,240,256]{2,1,0:T(8,128)(2,1...) custom-call(s32[7]{0:T(128)} %stack.40.refs_1_.refs_0_, ...), custom_call_target="tpu_custom_call", output_to_operand_aliasing={{5}: (9, {}), {6}: (10, {})} | custom-call | flops 14000000000 | bytes 16000000 | tf_op jit(solution)/shard_map/backward_group/pallas_call | solution.py:140
  231.0 11.7 %last_part.1 = (bf16[2048,512]{1,0:T(8,128)(2,1)}, f32[16,512]{1,0:T(8,128)}, bf16[240,512]{1,0:T(8,128)(2,1)}, f32[240,512]{1,0:T(8,128)}, f32[240,768]{1,0:T(8,128)}, /*index=5*/bf16[240,256]{1,0:T(8,128)(2,1)}) custom-call(bf16[2048,512]{1,0:T(8,128)(2,1)} %bitcast.120, ...), custom_call_target="tpu_custom_call", output_to_operand_aliasing={{2}: (13, {}), {3}: (14, {}), {4}: (15, {}), {5}: (16, {})} | custom-call | flops 4300000256 | bytes 20000000 | tf_op jit(solution)/shard_map/last_part/pallas_call | solution.py:140
  247.6 2.5 collective-permute-start.36
  256.8 6.5 %collective-permute-start.37 = (bf16[256,256]{1,0:T(8,128)(2,1)S(1)}, bf16[256,256]{1,0:T(8,128)(2,1)S(1)}, u32[]{:S(2)}, u32[]{:S(2)}) collective-permute-start(bf16[256,256]{1,0:T(8,128)(2,1)S(1)} %fusion.15), channel_id=1, source_target_pairs={{0,24},{24,0},{1,25},{25,1},{2,26},{26,2},{3,27},{27,3},{4,28},{28... | collective-permute-start | bytes 393224 | tf_op jit(solution)/shard_map/ppermute | solution.py:812
  263.5 3.7 %collective-permute-done.38 = bf16[256,256]{1,0:T(8,128)(2,1)S(1)} collective-permute-done((bf16[256,256]{1,0:T(8,128)(2,1)S(1)}, bf16[256,256]{1,0:T(8,128)(2,1)S(1)}, u32[]{:S(2)}, u32[]{:S(2)}) %collective-permute-start.38) | collective-permute-done | bytes 131104 | tf_op jit(solution)/shard_map/ppermute | solution.py:812
  (171 shorter events, 55.8 us)
Async XLA Ops:
  11.8 13.1 %collective-permute-start.5 = (bf16[256,512]{1,0:T(8,128)(2,1)S(1)}, bf16[256,512]{1,0:T(8,128)(2,1)S(1)}, u32[]{:S(2)}, u32[]{:S(2)}) collective-permute-start(bf16[256,512]{1,0:T(8,128)(2,1)S(1)} %broadcast_select_fusion), channel_id=1, source_target_pairs={{0,8},{8,0},{16,24},{24,16},{1,9},{9,1},{17,25},{25,17},{2,10},{10... | collective-permute-start | bytes 786440 | tf_op jit(solution)/shard_map/ppermute | solution.py:812
  16.2 15.0 %collective-permute-start.1 = (bf16[1,240,512]{2,1,0:T(8,128)(2,1)S(1)}, bf16[1,240,512]{2,1,0:T(8,128)(2,1)S(1)}, u32[]{:S(2)}, u32[]{:S(2)}) collective-permute-start(bf16[1,240,512]{2,1,0:T(8,128)(2,1)S(1)} %convert_element_type.312), channel_id=1, source_target_pairs={{0,4},{4,0},{1,5},{5,1},{2,6},{6,2},{3,7},{7,3},{8,12},{12,8},{9,1... | collective-permute-start | bytes 737288 | tf_op jit(solution)/shard_map/ppermute | solution.py:812
  17.8 10.9 %collective-permute-start = (bf16[1,240,512]{2,1,0:T(8,128)(2,1)S(1)}, bf16[1,240,512]{2,1,0:T(8,128)(2,1)S(1)}, u32[]{:S(2)}, u32[]{:S(2)}) collective-permute-start(bf16[1,240,512]{2,1,0:T(8,128)(2,1)S(1)} %convert_element_type.312), channel_id=1, source_target_pairs={{0,2},{2,0},{1,3},{3,1},{4,6},{6,4},{5,7},{7,5},{8,10},{10,8},{9,1... | collective-permute-start | bytes 737288 | tf_op jit(solution)/shard_map/ppermute | solution.py:812
  27.6 12.7 %collective-permute-start.8 = (bf16[1,256,512]{2,1,0:T(8,128)(2,1)S(1)}, bf16[1,256,512]{2,1,0:T(8,128)(2,1)S(1)}, u32[]{:S(2)}, u32[]{:S(2)}) collective-permute-start(bf16[1,256,512]{2,1,0:T(8,128)(2,1)S(1)} %maximum_bitcast_fusion), channel_id=1, source_target_pairs={{0,4},{4,0},{1,5},{5,1},{2,6},{6,2},{3,7},{7,3},{8,12},{12,8},{9,1... | collective-permute-start | bytes 786440 | tf_op jit(solution)/shard_map/ppermute | solution.py:812
  28.1 12.1 %collective-permute-start.7 = (bf16[1,256,512]{2,1,0:T(8,128)(2,1)S(1)}, bf16[1,256,512]{2,1,0:T(8,128)(2,1)S(1)}, u32[]{:S(2)}, u32[]{:S(2)}) collective-permute-start(bf16[1,256,512]{2,1,0:T(8,128)(2,1)S(1)} %maximum_bitcast_fusion), channel_id=1, source_target_pairs={{0,2},{2,0},{1,3},{3,1},{4,6},{6,4},{5,7},{7,5},{8,10},{10,8},{9,1... | collective-permute-start | bytes 786440 | tf_op jit(solution)/shard_map/ppermute | solution.py:812
  28.7 14.1 %collective-permute-start.2 = (bf16[1,240,512]{2,1,0:T(8,128)(2,1)S(1)}, bf16[1,240,512]{2,1,0:T(8,128)(2,1)S(1)}, u32[]{:S(2)}, u32[]{:S(2)}) collective-permute-start(bf16[1,240,512]{2,1,0:T(8,128)(2,1)S(1)} %convert_element_type.312), channel_id=1, source_target_pairs={{0,6},{2,4},{4,2},{6,0},{1,7},{3,5},{5,3},{7,1},{8,14},{10,12},{12... | collective-permute-start | bytes 737288 | tf_op jit(solution)/shard_map/ppermute | solution.py:812
  44.5 33.4 %collective-permute-start.14 = (bf16[2,240,512]{2,1,0:T(8,128)(2,1)}, bf16[2,240,512]{2,1,0:T(8,128)(2,1)}, u32[]{:S(2)}, u32[]{:S(2)}) collective-permute-start(bf16[2,240,512]{2,1,0:T(8,128)(2,1)} %pad_maximum_fusion.2.refs_12_), channel_id=1, source_target_pairs={{0,6},{2,4},{4,2},{6,0},{1,7},{3,5},{5,3},{7,1},{8,14},{10,12},{12... | collective-permute-start | bytes 1474568 | tf_op jit(solution)/shard_map/ppermute | solution.py:812
  47.0 30.9 %collective-permute-start.13 = (bf16[2,240,512]{2,1,0:T(8,128)(2,1)}, bf16[2,240,512]{2,1,0:T(8,128)(2,1)}, u32[]{:S(2)}, u32[]{:S(2)}) collective-permute-start(bf16[2,240,512]{2,1,0:T(8,128)(2,1)} %pad_maximum_fusion.2.refs_12_), channel_id=1, source_target_pairs={{0,4},{4,0},{1,5},{5,1},{2,6},{6,2},{3,7},{7,3},{8,12},{12,8},{9,1... | collective-permute-start | bytes 1474568 | tf_op jit(solution)/shard_map/ppermute | solution.py:812
  47.6 29.2 %collective-permute-start.12 = (bf16[2,240,512]{2,1,0:T(8,128)(2,1)}, bf16[2,240,512]{2,1,0:T(8,128)(2,1)}, u32[]{:S(2)}, u32[]{:S(2)}) collective-permute-start(bf16[2,240,512]{2,1,0:T(8,128)(2,1)} %pad_maximum_fusion.2.refs_12_), channel_id=1, source_target_pairs={{0,2},{2,0},{1,3},{3,1},{4,6},{6,4},{5,7},{7,5},{8,10},{10,8},{9,1... | collective-permute-start | bytes 1474568 | tf_op jit(solution)/shard_map/ppermute | solution.py:812
  138.6 14.6 %collective-permute-start.16 = (bf16[4,240,512]{2,1,0:T(8,128)(2,1)}, bf16[4,240,512]{2,1,0:T(8,128)(2,1)}, u32[]{:S(2)}, u32[]{:S(2)}) collective-permute-start(bf16[4,240,512]{2,1,0:T(8,128)(2,1)} %get-tuple-element.80), channel_id=1, source_target_pairs={{0,1},{1,0},{2,3},{3,2},{4,5},{5,4},{6,7},{7,6},{8,9},{9,8},{10,11... | collective-permute-start | bytes 2949128 | tf_op jit(solution)/shard_map/ppermute | solution.py:812
  139.0 15.7 %collective-permute-start.17 = (bf16[4,240,512]{2,1,0:T(8,128)(2,1)}, bf16[4,240,512]{2,1,0:T(8,128)(2,1)S(1)}, u32[]{:S(2)}, u32[]{:S(2)}) collective-permute-start(bf16[4,240,512]{2,1,0:T(8,128)(2,1)} %get-tuple-element.81), channel_id=1, source_target_pairs={{0,1},{1,0},{2,3},{3,2},{4,5},{5,4},{6,7},{7,6},{8,9},{9,8},{10,11... | collective-permute-start | bytes 2949128 | tf_op jit(solution)/shard_map/ppermute | solution.py:812
  150.3 33.7 %collective-permute-start.21 = (bf16[4,240,512]{2,1,0:T(8,128)(2,1)}, bf16[4,240,512]{2,1,0:T(8,128)(2,1)S(1)}, u32[]{:S(2)}, u32[]{:S(2)}) collective-permute-start(bf16[4,240,512]{2,1,0:T(8,128)(2,1)} %get-tuple-element.92), channel_id=1, source_target_pairs={{0,1},{1,0},{2,3},{3,2},{4,5},{5,4},{6,7},{7,6},{8,9},{9,8},{10,11... | collective-permute-start | bytes 2949128 | tf_op jit(solution)/shard_map/ppermute | solution.py:812
  154.9 30.0 %collective-permute-start.20 = (bf16[240,1024]{1,0:T(8,128)(2,1)S(1)}, bf16[240,1024]{1,0:T(8,128)(2,1)S(1)}, u32[]{:S(2)}, u32[]{:S(2)}) collective-permute-start(bf16[240,1024]{1,0:T(8,128)(2,1)S(1)} %add_convert_fusion), channel_id=1, source_target_pairs={{0,6},{2,4},{4,2},{6,0},{1,7},{3,5},{5,3},{7,1},{8,14},{10,12},{12... | collective-permute-start | bytes 1474568 | tf_op jit(solution)/shard_map/ppermute | solution.py:812
  158.3 26.6 %collective-permute-start.18 = (bf16[240,1024]{1,0:T(8,128)(2,1)}, bf16[240,1024]{1,0:T(8,128)(2,1)}, u32[]{:S(2)}, u32[]{:S(2)}) collective-permute-start(bf16[240,1024]{1,0:T(8,128)(2,1)} %add_convert_fusion.2), channel_id=1, source_target_pairs={{0,2},{2,0},{1,3},{3,1},{4,6},{6,4},{5,7},{7,5},{8,10},{10,8},{9,1... | collective-permute-start | bytes 1474568 | tf_op jit(solution)/shard_map/ppermute | solution.py:812
  159.7 25.2 %collective-permute-start.19 = (bf16[240,1024]{1,0:T(8,128)(2,1)}, bf16[240,1024]{1,0:T(8,128)(2,1)}, u32[]{:S(2)}, u32[]{:S(2)}) collective-permute-start(bf16[240,1024]{1,0:T(8,128)(2,1)} %add_convert_fusion.1), channel_id=1, source_target_pairs={{0,4},{4,0},{1,5},{5,1},{2,6},{6,2},{3,7},{7,3},{8,12},{12,8},{9,1... | collective-permute-start | bytes 1474568 | tf_op jit(solution)/shard_map/ppermute | solution.py:812
  186.6 38.2 %collective-permute-start.26 = (bf16[240,1024]{1,0:T(8,128)(2,1)S(1)}, bf16[240,1024]{1,0:T(8,128)(2,1)S(1)}, u32[]{:S(2)}, u32[]{:S(2)}) collective-permute-start(bf16[240,1024]{1,0:T(8,128)(2,1)S(1)} %get-tuple-element.113), channel_id=1, source_target_pairs={{0,16},{8,24},{1,17},{9,25},{2,18},{10,26},{3,19},{11,27},{4,20},{... | collective-permute-start | bytes 1474568 | tf_op jit(solution)/shard_map/ppermute | solution.py:812
  193.0 28.2 %collective-permute-start.23 = (bf16[240,768]{1,0:T(8,128)(2,1)}, bf16[240,768]{1,0:T(8,128)(2,1)S(1)}, u32[]{:S(2)}, u32[]{:S(2)}) collective-permute-start(bf16[240,768]{1,0:T(8,128)(2,1)} %get-tuple-element.119), channel_id=1, source_target_pairs={{0,2},{2,0},{1,3},{3,1},{4,6},{6,4},{5,7},{7,5},{8,10},{10,8},{9,1... | collective-permute-start | bytes 1105928 | tf_op jit(solution)/shard_map/ppermute | solution.py:812
  194.6 26.7 %collective-permute-start.24 = (bf16[240,768]{1,0:T(8,128)(2,1)}, bf16[240,768]{1,0:T(8,128)(2,1)S(1)}, u32[]{:S(2)}, u32[]{:S(2)}) collective-permute-start(bf16[240,768]{1,0:T(8,128)(2,1)} %get-tuple-element.120), channel_id=1, source_target_pairs={{0,4},{4,0},{1,5},{5,1},{2,6},{6,2},{3,7},{7,3},{8,12},{12,8},{9,1... | collective-permute-start | bytes 1105928 | tf_op jit(solution)/shard_map/ppermute | solution.py:812
  196.1 25.2 %collective-permute-start.25 = (bf16[240,768]{1,0:T(8,128)(2,1)}, bf16[240,768]{1,0:T(8,128)(2,1)}, u32[]{:S(2)}, u32[]{:S(2)}) collective-permute-start(bf16[240,768]{1,0:T(8,128)(2,1)} %get-tuple-element.121), channel_id=1, source_target_pairs={{0,6},{2,4},{4,2},{6,0},{1,7},{3,5},{5,3},{7,1},{8,14},{10,12},{12... | collective-permute-start | bytes 1105928 | tf_op jit(solution)/shard_map/ppermute | solution.py:812
  223.4 20.8 %collective-permute-start.31 = (bf16[240,768]{1,0:T(8,128)(2,1)S(1)}, bf16[240,768]{1,0:T(8,128)(2,1)S(1)}, u32[]{:S(2)}, u32[]{:S(2)}) collective-permute-start(bf16[240,768]{1,0:T(8,128)(2,1)S(1)} %get-tuple-element.111), channel_id=1, source_target_pairs={{16,0},{24,8},{17,1},{25,9},{18,2},{26,10},{19,3},{27,11},{20,4},{... | collective-permute-start | bytes 1105928 | tf_op jit(solution)/shard_map/ppermute | solution.py:812
  227.5 15.2 %collective-permute-start.28 = (bf16[240,256]{1,0:T(8,128)(2,1)S(1)}, bf16[240,256]{1,0:T(8,128)(2,1)S(1)}, u32[]{:S(2)}, u32[]{:S(2)}) collective-permute-start(bf16[240,256]{1,0:T(8,128)(2,1)S(1)} %get-tuple-element.115), channel_id=1, source_target_pairs={{0,2},{2,0},{1,3},{3,1},{4,6},{6,4},{5,7},{7,5},{8,10},{10,8},{9,1... | collective-permute-start | bytes 368648 | tf_op jit(solution)/shard_map/ppermute | solution.py:812
  229.0 13.7 %collective-permute-start.29 = (bf16[240,256]{1,0:T(8,128)(2,1)S(1)}, bf16[240,256]{1,0:T(8,128)(2,1)S(1)}, u32[]{:S(2)}, u32[]{:S(2)}) collective-permute-start(bf16[240,256]{1,0:T(8,128)(2,1)S(1)} %get-tuple-element.116), channel_id=1, source_target_pairs={{0,4},{4,0},{1,5},{5,1},{2,6},{6,2},{3,7},{7,3},{8,12},{12,8},{9,1... | collective-permute-start | bytes 368648 | tf_op jit(solution)/shard_map/ppermute | solution.py:812
  230.5 12.2 %collective-permute-start.30 = (bf16[240,256]{1,0:T(8,128)(2,1)S(1)}, bf16[240,256]{1,0:T(8,128)(2,1)S(1)}, u32[]{:S(2)}, u32[]{:S(2)}) collective-permute-start(bf16[240,256]{1,0:T(8,128)(2,1)S(1)} %get-tuple-element.117), channel_id=1, source_target_pairs={{0,6},{2,4},{4,2},{6,0},{1,7},{3,5},{5,3},{7,1},{8,14},{10,12},{12... | collective-permute-start | bytes 368648 | tf_op jit(solution)/shard_map/ppermute | solution.py:812
  255.5 11.7 %collective-permute-start.38 = (bf16[256,256]{1,0:T(8,128)(2,1)S(1)}, bf16[256,256]{1,0:T(8,128)(2,1)S(1)}, u32[]{:S(2)}, u32[]{:S(2)}) collective-permute-start(bf16[256,256]{1,0:T(8,128)(2,1)S(1)} %fusion.15), channel_id=1, source_target_pairs={{8,24},{16,0},{9,25},{17,1},{10,26},{18,2},{11,27},{19,3},{12,28},... | collective-permute-start | bytes 393224 | tf_op jit(solution)/shard_map/ppermute | solution.py:812
  (37 other events, 206.1 us)
